TPU v7x, 32 devices: a whole 2x2x4 slice. The times are simulated.
32 devices in a mesh: gx: 8 (over z, x), gy: 4 (over y, core).
Axes of the slice: x: 2, y: 2, z: 4, core: 2. Of those that a mesh axis runs over, the one named last changes fastest.
Arguments:
- blocks: float32 [8, 4, 64, 4, 128], P('gx', 'gy'), may hold values from 0 to 1, as said below
- active_counts: int32 [8, 4], P('gx', 'gy'), may hold values from 1 to 32, as said below
- pair_lists: int32 [8, 4, 32, 16], P('gx', 'gy'), may hold values from 0 to 575
- cell_ids: int32 [8, 4, 64], P('gx', 'gy'), may hold values from 0 to 15, as said below
Outputs:
- accel: float32 [8, 4, 32, 3, 128], P('gx', 'gy')
Inputs may be any that keep to these rules, and one draw needn't show every extreme that they name: `active_counts`: every domain has at least one active block and some domain has 32; the active blocks are the first ones of the domain. `pair_lists`: entry (3 a + b) * 64 + n names block n of the domain a - 1 steps along gx and b - 1 steps along gy, with wrap around; a list may repeat a block or name the target block itself. `cell_ids`: A block of domain (i, j) lies in one of the 2 cells (g * 2 + h) with g = (i // 2) * (4 // 2) + j // 2. `blocks`: coordinates lie in [0, 1); masses are positive.
All inputs are finite; a program needn't handle non-finite values.
Results may differ from a plain program's by a relative error of at most 0.0003.
Values sent between devices are 32-bit elements; how exact they have to be, the bound alone decides.
No kernel may reach another device: no remote copies, remote signals or barrier semaphores. Data moves between devices by JAX's collectives and lax.ppermute only.
A program may use at most 64 MiB of HBM per device.

v0:
```python
import functools
import math

import jax
import jax.numpy as jnp
from jax import lax
from jax.experimental import pallas as pl
from jax.experimental.pallas import tpu as pltpu
from jax.sharding import PartitionSpec as P

SUBC = 2
F32 = jnp.float32
BF16 = jnp.bfloat16

soft_near = 0.05
soft_far = 1.0
middle = 0.5


def swap(block, axis, odd):
    count = lax.axis_size(axis)
    pairs = []
    for low in range(odd, count, 2):
        high = (low + 1) % count
        pairs += [(low, high), (high, low)]
    return lax.ppermute(block, axis, pairs)


def exchange(values, axis, step):
    return lax.ppermute(values, axis, [(i, i ^ step) for i in range(lax.axis_size(axis))])


def split_slots(slots, together):
    groups = slots // together
    cuts = [0, max(1, groups // 4), groups]
    return [(a * together, (b - a) * together) for a, b in zip(cuts, cuts[1:]) if b > a]


def near_cost(slots, entries, width):
    pairs = slots * entries * width * width
    return pl.CostEstimate(flops=20 * pairs, bytes_accessed=3 * slots * width * 4, transcendentals=pairs)


def split3(v):
    high = v.astype(BF16).astype(F32)
    rest = v - high
    mid = rest.astype(BF16).astype(F32)
    return high, mid, rest - mid


def roll(v, step):
    return pltpu.roll(v, step, 0)


def halves(low_half, pairs):
    upper = [jnp.where(low_half, first, roll(second, 4)) for first, second in pairs]
    lower = [jnp.where(low_half, roll(first, 4), second) for first, second in pairs]
    return [jnp.concatenate(rows, axis=0).astype(BF16) for rows in (upper, lower)]


def square_norm(is_mass, centred):
    square = jnp.where(is_mass, 0.0, centred)
    square = square * square
    return (roll(square, 1) + roll(square, 2)) + roll(square, 3)


def source_tile(tile, moved, is_mass, low_half):
    zero = jnp.zeros_like(tile)
    centred = (tile + moved) - jnp.where(is_mass, 0.0, middle)
    rows = jnp.where(is_mass, square_norm(is_mass, centred), -2.0 * centred)
    high, mid, low = split3(rows)
    high_1, mid_1 = jnp.where(is_mass, 1.0, high), jnp.where(is_mass, 1.0, mid)
    features = halves(low_half, [(high, high_1), (high_1, mid), (mid_1, low), (zero, zero)])
    mass = jnp.where(is_mass, tile, 0.0)
    mass = (mass + roll(mass, 7)) + (roll(mass, 6) + roll(mass, 5))
    high, mid, low = split3(jnp.where(is_mass, 1.0, centred) * mass)
    return features, halves(low_half, [(high, mid), (low, zero)])


def target_tile(tile, is_mass, low_half):
    zero = jnp.zeros_like(tile)
    centred = tile - middle
    norm = square_norm(is_mass, centred) + soft_near * soft_near
    high, mid, low = split3(jnp.where(is_mass, norm, centred))
    one_high = jnp.where(is_mass, 1.0, high)
    high_mid = jnp.where(is_mass, high, mid)
    mid_low = jnp.where(is_mass, mid, low)
    low_mid = jnp.where(is_mass, low, mid)
    return halves(low_half, [(one_high, high_mid), (mid_low, one_high), (low_mid, one_high), (zero, zero)])


def mark(blocks, ids_in, out, ids, sems, *, half_gy):
    rows, width = blocks.shape
    copies = [
        pltpu.make_async_copy(ids_in, ids, sems.at[0]),
        pltpu.make_async_copy(blocks, out.at[pl.ds(0, rows), :], sems.at[1]),
    ]
    for copy in copies:
        copy.start()
    for copy in copies:
        copy.wait()
    first = (lax.axis_index("gx") // 2 * half_gy + lax.axis_index("gy") // 2) * SUBC
    count = ids.shape[1]
    line = lax.broadcasted_iota(jnp.int32, (8, count), 0)
    member = jnp.where(ids[...] - first == line, 1.0, 0.0)
    mass = out[pl.ds(3, count, stride=4), :]
    sums = jnp.dot(member, mass, preferred_element_type=F32, precision=lax.Precision.HIGHEST)
    sums = jnp.sum(sums, axis=1, keepdims=True)
    shape = (out.shape[0] - rows, width)
    cell = lax.broadcasted_iota(jnp.int32, shape, 0) * width + lax.broadcasted_iota(jnp.int32, shape, 1)
    values = jnp.zeros(shape, F32)
    for h in range(SUBC):
        values = jnp.where(cell == first + h, jnp.broadcast_to(sums[h : h + 1], shape), values)
    out[rows:, :] = values


def add_sources(pieces, places, feature, moment, count_blocks):
    width = feature.shape[2]
    even_x, even_y = 1 - lax.axis_index("gx") % 2, 1 - lax.axis_index("gy") % 2
    line = lax.broadcasted_iota(jnp.int32, (8, width), 0)
    is_mass, low_half = line % 4 == 3, line < 4
    is_x, is_y = line % 4 == 0, line % 4 == 1
    tiles = count_blocks // 2
    for piece, (row, col) in zip(pieces, places):
        a = (1, 2 * even_x, 2 - 2 * even_x)[row]
        b = (1, 2 * even_y, 2 - 2 * even_y)[col]
        step_a = jnp.asarray(a - 1, F32)
        step_b = jnp.asarray(b - 1, F32)
        moved = jnp.where(is_x, step_a, jnp.where(is_y, step_b, 0.0))

        def some_tiles(group, carry, piece=piece, base=(3 * a + b) * tiles, moved=moved):
            for u in range(2):
                at = group * 2 + u
                tile = piece[pl.ds(pl.multiple_of(at * 8, 8), 8), :]
                features, moments = source_tile(tile, moved, is_mass, low_half)
                for half in range(2):
                    feature[2 * (base + at) + half] = features[half]
                    moment[2 * (base + at) + half] = moments[half]
            return carry

        lax.fori_loop(0, tiles // 2, some_tiles, 0)


def start_rows(*refs, places, count_blocks):
    pieces, (feature, moment, target, centre) = refs[:-4], refs[-4:]
    slots, width = centre.shape[1:]
    own = pieces[0]
    line = lax.broadcasted_iota(jnp.int32, (8, width), 0)
    is_mass, low_half = line % 4 == 3, line < 4

    def one_target(pair, carry):
        tile = own[pl.ds(pl.multiple_of(pair * 8, 8), 8), :]
        for half, value in enumerate(target_tile(tile, is_mass, low_half)):
            target[2 * pair + half] = value
        return carry

    lax.fori_loop(0, slots // 2, one_target, 0)
    for c in range(3):
        centre[c] = own[pl.ds(c, slots, stride=4), :] - middle
    add_sources(pieces, places, feature, moment, count_blocks)


def more_rows(feature_in, moment_in, *refs, places, count_blocks):
    pieces, (feature, moment) = refs[:-2], refs[-2:]
    add_sources(pieces, places, feature, moment, count_blocks)


def last_rows(feature_in, moment_in, *refs, places, count_blocks, here, there):
    pieces, (feature, moment, here_mass, there_mass) = refs[:-4], refs[-4:]
    width = feature.shape[2]
    for row in range(here_mass.shape[0] // width):
        for out, members in ((here_mass, here), (there_mass, there)):
            values = [pieces[k][count_blocks * 4 + row, :] for k in members]
            out[pl.ds(row * width, width)] = functools.reduce(jnp.add, values)
    add_sources(pieces[: len(places)], places, feature, moment, count_blocks)


def pair_sums(first, count, limit, lists, feature, moment, target, centre, out, together):
    entries = lists.shape[0]

    def some_slots(group, carry):
        for u in range(together):
            at = group * together + u
            slot = first + at
            near = target[slot]
            sums = jnp.zeros((moment.shape[1], moment.shape[2]), F32)
            for k in range(0, entries, 2):
                one, two = lists[k, slot], lists[k + 1, slot]
                here = jnp.concatenate([feature[one], feature[two]], axis=1)
                parts = jnp.concatenate([moment[one], moment[two]], axis=1)
                dist_sq = lax.dot_general(here, near, (((0,), (0,)), ((), ())), preferred_element_type=F32)
                inverse = lax.rsqrt(dist_sq)
                weight = inverse * inverse * inverse
                high = weight.astype(BF16)
                low = (weight - high.astype(F32)).astype(BF16)
                sums += jnp.dot(parts, high, preferred_element_type=F32)
                sums += jnp.dot(parts, low, preferred_element_type=F32)
            sums = (sums[0:4] + sums[4:8]) + sums[8:12]
            for c in range(3):
                own = centre[c, pl.ds(slot, 1), :]
                out[c, pl.ds(at, 1), :] = sums[c : c + 1] - own * sums[3:4]
        return carry

    groups = jnp.clip(limit[0, 0] - first + together - 1, 0, count) // together
    lax.fori_loop(0, groups, some_slots, 0)


def near_forces(limit_in, lists_in, tie, feature_in, moment_in, target, centre, *refs, places, count_blocks, first, together):
    pieces, (out, feature, moment, lists, limit, sems) = refs[:-6], refs[-6:]
    copies = [pltpu.make_async_copy(lists_in, lists, sems.at[0]), pltpu.make_async_copy(limit_in, limit, sems.at[1])]
    for copy in copies:
        copy.start()
    add_sources(pieces, places, feature, moment, count_blocks)
    for copy in copies:
        copy.wait()
    pair_sums(first, out.shape[1], limit, lists, feature, moment, target, centre, out, together)


def add_far(limit_in, some_mass, more_mass, centre_in, *refs, half_gy, total, unroll):
    nears, out, near, centre, masses, limit, sems = refs[:-6], *refs[-6:]
    slots, width = out.shape[1:]
    copies = [
        pltpu.make_async_copy(some_mass, masses.at[0], sems.at[0]),
        pltpu.make_async_copy(more_mass, masses.at[1], sems.at[1]),
        pltpu.make_async_copy(centre_in, centre, sems.at[2]),
        pltpu.make_async_copy(limit_in, limit, sems.at[3]),
    ]
    at = 0
    for k, piece in enumerate(nears):
        count = piece.shape[1]
        copies.append(pltpu.make_async_copy(piece, near.at[:, pl.ds(at, count), :], sems.at[4 + k]))
        at += count
    for copy in copies:
        copy.start()
    for copy in copies:
        copy.wait()
    corner = (lax.axis_index("gx").astype(F32) + middle, lax.axis_index("gy").astype(F32) + middle, middle)
    position = [centre[c] + corner[c] for c in range(3)]

    def cells(step, carry):
        for u in range(unroll):
            cell = step * unroll + u
            group, sub_cell = cell // SUBC, cell % SUBC
            centre = (
                (2 * (group // half_gy) + 1).astype(F32),
                (2 * (group % half_gy) + 1).astype(F32),
                (sub_cell.astype(F32) + 0.5) * (1.0 / SUBC),
            )
            offset = [centre[c] - position[c] for c in range(3)]
            dist_sq = (offset[0] * offset[0] + offset[1] * offset[1]) + offset[2] * offset[2]
            inverse = lax.rsqrt(dist_sq + soft_far * soft_far)
            weight = (masses[0, cell] + masses[1, cell]) * (inverse * inverse * inverse)
            carry = tuple(carry[c] + weight * offset[c] for c in range(3))
        return carry

    far = lax.fori_loop(0, total // unroll, cells, tuple(jnp.zeros_like(v) for v in position))
    active = lax.broadcasted_iota(jnp.int32, (slots, width), 0) < limit[0, 0]
    for c in range(3):
        out[c] = jnp.where(active, near[c] + far[c], 0.0)


def body(blocks, active_counts, pair_lists, cell_ids):
    count_blocks, width = blocks.shape[2], blocks.shape[4]
    slots, entries = pair_lists.shape[2:]
    half_gy = lax.axis_size("gy") // 2
    total = lax.axis_size("gx") // 2 * half_gy * SUBC
    own = blocks.reshape(count_blocks * 4, width)
    smem = pl.BlockSpec(memory_space=pltpu.SMEM)
    vmem = pl.BlockSpec(memory_space=pltpu.VMEM)

    lines = -(-total // width)
    rows = count_blocks * 4
    hbm = pl.BlockSpec(memory_space=pl.ANY)
    marked = pl.pallas_call(
        functools.partial(mark, half_gy=half_gy),
        out_shape=jax.ShapeDtypeStruct((rows + 8 * -(-lines // 8), width), F32),
        in_specs=[hbm] * 2,
        out_specs=vmem,
        scratch_shapes=[pltpu.VMEM((1, count_blocks), jnp.int32), pltpu.SemaphoreType.DMA((2,))],
        compiler_params=pltpu.CompilerParams(vmem_limit_bytes=2 * 2**20),
    )(own, cell_ids[0])
    lists = pair_lists[0, 0].T

    first_x = swap(marked, "gx", 0)
    second_y = swap(marked, "gy", 1)
    first_y = swap(marked, "gy", 0)
    second_x = swap(lax.optimization_barrier((own, marked))[0], "gx", 1)
    row_params = dict(
        compiler_params=pltpu.CompilerParams(vmem_limit_bytes=16 * 2**20),
        cost_estimate=pl.CostEstimate(flops=1, bytes_accessed=1, transcendentals=0),
    )
    table = list(pl.pallas_call(
        functools.partial(start_rows, places=[(0, 0)], count_blocks=count_blocks),
        out_shape=[
            jax.ShapeDtypeStruct((9 * count_blocks, 32, width), BF16),
            jax.ShapeDtypeStruct((9 * count_blocks, 16, width), BF16),
            jax.ShapeDtypeStruct((slots, 32, width), BF16),
            jax.ShapeDtypeStruct((3, slots, width), F32),
        ],
        in_specs=[vmem],
        out_specs=[vmem] * 4,
        **row_params,
    )(marked))

    second_x = second_x
    first_x = lax.optimization_barrier((first_x, table[3]))[0]
    first_xy = swap(first_x, "gy", 0)
    first_xyy = swap(first_x, "gy", 1)

    table[:2] = pl.pallas_call(
        functools.partial(more_rows, places=[(1, 0), (0, 1), (0, 2)], count_blocks=count_blocks),
        out_shape=table[:2],
        in_specs=[vmem] * 5,
        out_specs=[vmem] * 2,
        input_output_aliases={0: 0, 1: 1},
        **row_params,
    )(*table[:2], first_x, first_y, second_y)

    second_xy = swap(second_x, "gy", 0)
    second_xyy = swap(second_x, "gy", 1)
    more = [first_xy, second_x, second_xy, first_xyy, marked, first_x, first_y, second_y]
    *rows_now, here_mass, there_mass = pl.pallas_call(
        functools.partial(
            last_rows,
            places=[(1, 1), (2, 0), (2, 1), (1, 2)],
            count_blocks=count_blocks,
            here=(0, 4, 5, 6),
            there=(3, 7),
        ),
        out_shape=[*table[:2]] + [jax.ShapeDtypeStruct((lines * width,), F32)] * 2,
        in_specs=[vmem] * (2 + len(more)),
        out_specs=[vmem] * 4,
        input_output_aliases={0: 0, 1: 1},
        **row_params,
    )(*table[:2], *more)
    table = [*rows_now, *table[2:]]
    late, late_places = [second_xyy], [(2, 2)]

    together = math.gcd(slots, 8)
    ranges = split_slots(slots, together)

    def near_part(k, tie, table):
        first, count = ranges[k]
        pieces, places = (late, late_places) if k == 0 else ([], [])
        near, *rows = pl.pallas_call(
            functools.partial(
                near_forces, places=places, count_blocks=count_blocks, first=first, together=math.gcd(count, 12 if count % 12 == 0 else 8)
            ),
            out_shape=[jax.ShapeDtypeStruct((3, count, width), F32), *table[:2]],
            in_specs=[hbm] * 3 + [vmem] * (4 + len(pieces)),
            out_specs=[vmem] * 3,
            scratch_shapes=[
                pltpu.SMEM((entries, slots), jnp.int32),
                pltpu.SMEM((1, 1), jnp.int32),
                pltpu.SemaphoreType.DMA((2,)),
            ],
            input_output_aliases={3: 1, 4: 2},
            compiler_params=pltpu.CompilerParams(vmem_limit_bytes=24 * 2**20),
            cost_estimate=near_cost(count, entries, width),
        )(active_counts, lists, tie, *table, *pieces)
        return near, [*rows, *table[2:]]

    if lax.axis_size("gy") == 4:
        there_mass = lax.optimization_barrier((there_mass, second_xyy))[0]
        values = (here_mass + there_mass) + exchange(there_mass, "gy", 1)
        steps = []
    else:
        values = here_mass
        steps = [("gy", 2 << k) for k in range((lax.axis_size("gy") // 2).bit_length() - 1)]
    steps += [("gx", 2 << k) for k in range((lax.axis_size("gx") // 2).bit_length() - 1)]
    nears, parts = [], (values, jnp.zeros_like(values))
    for k, (axis, step) in enumerate(steps):
        if nears:
            values = lax.optimization_barrier((values, nears[-1]))[0]
        other = exchange(values, axis, step)
        parts = (values, other)
        if k >= len(steps) - 2 and len(nears) < len(ranges):
            near, table = near_part(len(nears), values, table)
            nears.append(near)
        values = values + other
    while len(nears) < len(ranges):
        near, table = near_part(len(nears), parts[0], table)
        nears.append(near)

    result = pl.pallas_call(
        functools.partial(add_far, half_gy=half_gy, total=total, unroll=math.gcd(total, 16)),
        out_shape=jax.ShapeDtypeStruct((3, slots, width), F32),
        in_specs=[hbm] * (4 + len(nears)),
        out_specs=vmem,
        scratch_shapes=[
            pltpu.VMEM((3, slots, width), F32),
            pltpu.VMEM((3, slots, width), F32),
            pltpu.SMEM((2, lines * width), F32),
            pltpu.SMEM((1, 1), jnp.int32),
            pltpu.SemaphoreType.DMA((4 + len(nears),)),
        ],
        compiler_params=pltpu.CompilerParams(vmem_limit_bytes=4 * 2**20),
    )(active_counts, *parts, table[3], *nears)
    return result.transpose(1, 0, 2)[None, None]


def solution(mesh):
    in_specs = (
        P("gx", "gy", None, None, None),
        P("gx", "gy"),
        P("gx", "gy", None, None),
        P("gx", "gy", None),
    )
    out_specs = P("gx", "gy", None, None, None)
    return jax.shard_map(body, mesh=mesh, in_specs=in_specs, out_specs=out_specs, check_vma=False)
```

profile of v0, /device:TPU:0, one launch (start us, length us, event | category | flops | bytes accessed | tf_op | source)
XLA Modules:
  0.0 35.4 jit_solution(10916160056389295368)
XLA Ops:
  0.0 0.7 %copy-done.1 = s32[1,1,64]{2,1,0:T(1,128)S(1)} copy-done((s32[1,1,64]{2,1,0:T(1,128)S(1)}, s32[1,1,64]{2,1,0:T(1,128)}, u32[]{:S(2)}) %copy-start.1) | copy-done | bytes 280
  0.7 1.2 %shard_map.46.refs_0_.refs_4_ = f32[264,128]{1,0:T(8,128)S(1)} custom-call(f32[256,128]{1,0:T(8,128)} %bitcast.blocks, s32[1,64]{1,0:T(1,128)S(1)} %bitcast.10), custom_call_target="tpu_custom_call" | custom-call | tf_op jit(solution)/shard_map/pallas_call | solution.py:274
  1.8 3.0 %collective-permute-start = (f32[264,128]{1,0:T(8,128)S(1)}, f32[264,128]{1,0:T(8,128)S(1)}, u32[]{:S(2)}, u32[]{:S(2)}) collective-permute-start(f32[264,128]{1,0:T(8,128)S(1)} %shard_map.46.refs_0_.refs_4_), channel_id=1, source_target_pairs={{0,4},{4,0},{8,12},{12,8},{16,20},{20,16},{24,28},{28,24},{1,5},{5... | collective-permute-start | bytes 405512 | tf_op jit(solution)/shard_map/ppermute | solution.py:26
  4.8 0.0 collective-permute-start.1
  4.8 3.6 %collective-permute-start.4 = (f32[256,128]{1,0:T(8,128)}, f32[256,128]{1,0:T(8,128)S(1)}, u32[]{:S(2)}, u32[]{:S(2)}) collective-permute-start(f32[256,128]{1,0:T(8,128)} %bitcast.blocks), channel_id=1, source_target_pairs={{4,8},{8,4},{12,16},{16,12},{20,24},{24,20},{28,0},{0,28},{5,9},{9... | collective-permute-start | bytes 393224 | tf_op jit(solution)/shard_map/ppermute | solution.py:26
  8.4 1.4 %collective-permute-start.2 = (f32[264,128]{1,0:T(8,128)S(1)}, f32[264,128]{1,0:T(8,128)S(1)}, u32[]{:S(2)}, u32[]{:S(2)}) collective-permute-start(f32[264,128]{1,0:T(8,128)S(1)} %shard_map.46.refs_0_.refs_4_), channel_id=1, source_target_pairs={{1,2},{2,1},{3,0},{0,3},{5,6},{6,5},{7,4},{4,7},{9,10},{10,9},{11,... | collective-permute-start | bytes 405512 | tf_op jit(solution)/shard_map/ppermute | solution.py:26
  9.7 0.6 %shard_map.47 = (bf16[576,32,128]{2,1,0:T(8,128)(2,1)S(1)}, bf16[576,16,128]{2,1,0:T(8,128)(2,1)S(1)}, bf16[32,32,128]{2,1,0:T(8,128)(2,1)S(1)}, f32[3,32,128]{2,1,0:T(8,128)S(1)}) custom-call(f32[264,128]{1,0:T(8,128)S(1)} %shard_map.46.refs_0_.refs_4_), custom_call_target="tpu_custom_call" | custom-call | flops 1 | bytes 1 | tf_op jit(solution)/shard_map/pallas_call | solution.py:292
  10.4 0.1 collective-permute-done.refs_0_.refs_5_
  10.5 0.2 collective-permute-start.3
  10.8 1.4 %collective-permute-start.6 = (f32[264,128]{1,0:T(8,128)S(1)}, f32[264,128]{1,0:T(8,128)S(1)}, u32[]{:S(2)}, u32[]{:S(2)}) collective-permute-start(f32[264,128]{1,0:T(8,128)S(1)} %collective-permute-done.refs_0_.refs_5_), channel_id=1, source_target_pairs={{1,2},{2,1},{3,0},{0,3},{5,6},{6,5},{7,4},{4,7},{9,10},{10,9},{11,... | collective-permute-start | bytes 405512 | tf_op jit(solution)/shard_map/ppermute | solution.py:26
  12.1 1.5 %collective-permute-done.4.refs_1_ = f32[256,128]{1,0:T(8,128)S(1)} collective-permute-done((f32[256,128]{1,0:T(8,128)}, f32[256,128]{1,0:T(8,128)S(1)}, u32[]{:S(2)}, u32[]{:S(2)}) %collective-permute-start.4) | collective-permute-done | bytes 131104 | tf_op jit(solution)/shard_map/ppermute | solution.py:26
  13.6 0.0 collective-permute-start.5
  13.6 0.0 collective-permute-done.1.refs_1_.refs_6_
  13.6 1.6 %collective-permute-start.7 = (f32[256,128]{1,0:T(8,128)S(1)}, f32[256,128]{1,0:T(8,128)S(1)}, u32[]{:S(2)}, u32[]{:S(2)}) collective-permute-start(f32[256,128]{1,0:T(8,128)S(1)} %collective-permute-done.4.refs_1_), channel_id=1, source_target_pairs={{1,2},{2,1},{3,0},{0,3},{5,6},{6,5},{7,4},{4,7},{9,10},{10,9},{11,... | collective-permute-start | bytes 393224 | tf_op jit(solution)/shard_map/ppermute | solution.py:26
  15.3 0.0 collective-permute-done.2.refs_2_.refs_7_
  15.3 1.0 %shard_map.48 = (bf16[576,32,128]{2,1,0:T(8,128)(2,1)S(1)}, bf16[576,16,128]{2,1,0:T(8,128)(2,1)S(1)}) custom-call(bf16[576,32,128]{2,1,0:T(8,128)(2,1)S(1)} %get-tuple-element.23.feature_in, bf16[576,16,128]{2,1,0:T(8,128)(2,1)S(1)} %get-tuple-element.24.moment_in, ...), custom_call_target="tpu_custom_call", output_to_operand_aliasing={{0}: (0, {}), {1}: (1, {})} | custom-call | flops 1 | bytes 1 | tf_op jit(solution)/shard_map/pallas_call | solution.py:310
  16.3 0.0 copy-start
  16.3 0.0 collective-permute-done.5.refs_2_
  16.3 0.0 collective-permute-done.3.refs_0_
  16.4 0.5 %collective-permute-done.6.refs_3_ = f32[264,128]{1,0:T(8,128)S(1)} collective-permute-done((f32[264,128]{1,0:T(8,128)S(1)}, f32[264,128]{1,0:T(8,128)S(1)}, u32[]{:S(2)}, u32[]{:S(2)}) %collective-permute-start.6) | collective-permute-done | bytes 135200 | tf_op jit(solution)/shard_map/ppermute | solution.py:26
  16.9 1.4 %shard_map.49 = (bf16[576,32,128]{2,1,0:T(8,128)(2,1)S(1)}, bf16[576,16,128]{2,1,0:T(8,128)(2,1)S(1)}, f32[128]{0:T(128)S(1)}, f32[128]{0:T(128)S(1)}) custom-call(bf16[576,32,128]{2,1,0:T(8,128)(2,1)S(1)} %get-tuple-element.27.feature_in, bf16[576,16,128]{2,1,0:T(8,128)(2,1)S(1)} %get-tuple-element.28.moment_in, ...), custom_call_target="tpu_custom_call", output_to_operand_aliasing={{0}: (0, {}), {1}: (1, {})} | custom-call | flops 1 | bytes 1 | tf_op jit(solution)/shard_map/pallas_call | solution.py:322
  18.2 1.4 %collective-permute-done.7.refs_0_ = f32[256,128]{1,0:T(8,128)S(1)} collective-permute-done((f32[256,128]{1,0:T(8,128)S(1)}, f32[256,128]{1,0:T(8,128)S(1)}, u32[]{:S(2)}, u32[]{:S(2)}) %collective-permute-start.7) | collective-permute-done | bytes 131104 | tf_op jit(solution)/shard_map/ppermute | solution.py:26
  19.7 0.1 collective-permute-start.8
  20.5 0.3 collective-permute-done.8
  20.8 0.6 %collective-permute-start.9 = (f32[128]{0:T(128)S(1)}, f32[128]{0:T(128)S(1)}, u32[]{:S(2)}, u32[]{:S(2)}) collective-permute-start(f32[128]{0:T(128)S(1)} %add_add_fusion.tie), channel_id=1, source_target_pairs={{0,8},{4,12},{8,0},{12,4},{16,24},{20,28},{24,16},{28,20},{1,9},{5... | collective-permute-start | bytes 1544 | tf_op jit(solution)/shard_map/ppermute | solution.py:30
  21.4 0.0 copy-done
  21.4 3.2 %shard_map.50 = (f32[3,8,128]{2,1,0:T(8,128)S(1)}, bf16[576,32,128]{2,1,0:T(8,128)(2,1)S(1)}, bf16[576,16,128]{2,1,0:T(8,128)(2,1)S(1)}) custom-call(s32[1,1]{1,0:T(1,128)S(6)} %copy.21.limit_in, s32[16,32]{1,0:T(8,128)S(1)} %bitcast.8, f32[128]{0:T(128)S(1)} %add_add_fusion.tie, ...), custom_call_target="tpu_custom_call", output_to_operand_aliasing={{1}: (3, {}), {2}: (4, {})} | custom-call | flops 41943040 | bytes 12288 | tf_op jit(solution)/shard_map/pallas_call | solution.py:345
  24.7 0.0 collective-permute-done.9
  24.7 1.3 %collective-permute-start.10 = (f32[128]{0:T(128)S(1)}, f32[128]{0:T(128)S(1)}, u32[]{:S(2)}, u32[]{:S(2)}) collective-permute-start(f32[128]{0:T(128)S(1)} %add.11.tie.some_mass), channel_id=1, source_target_pairs={{0,16},{4,20},{8,24},{12,28},{16,0},{20,4},{24,8},{28,12},{1,17},{... | collective-permute-start | bytes 1544 | tf_op jit(solution)/shard_map/ppermute | solution.py:30
  26.0 8.0 %shard_map.51 = (f32[3,24,128]{2,1,0:T(8,128)S(1)}, bf16[576,32,128]{2,1,0:T(8,128)(2,1)S(1)}, bf16[576,16,128]{2,1,0:T(8,128)(2,1)S(1)}) custom-call(s32[1,1]{1,0:T(1,128)S(6)} %copy.21.limit_in, s32[16,32]{1,0:T(8,128)S(1)} %bitcast.9, f32[128]{0:T(128)S(1)} %add.11.tie.some_mass, ...), custom_call_target="tpu_custom_call", output_to_operand_aliasing={{1}: (3, {}), {2}: (4, {})} | custom-call | flops 125829120 | bytes 36864 | tf_op jit(solution)/shard_map/pallas_call | solution.py:345
  33.9 0.0 collective-permute-done.10.more_mass
  34.0 1.4 %shard_map.52 = f32[3,32,128]{2,1,0:T(8,128)} custom-call(s32[1,1]{1,0:T(1,128)S(6)} %copy.21.limit_in, f32[128]{0:T(128)S(1)} %add.11.tie.some_mass, f32[128]{0:T(128)S(1)} %collective-permute-done.10.more_mass, f32[3,32,128]{2,1,0:T(8,128)S(1)} %get-tuple-element.25.centre.centre_in, f32[3,8,128]{2,1,0:T(8,128)S(1)} %get-tuple-element.36.refs_0_, ...), custom_call_target="tpu_custom_call" | custom-call | tf_op jit(solution)/shard_map/pallas_call | solution.py:385
  (3 shorter events, 0.0 us)
Async XLA Ops:
  0.0 0.7 %copy-start.1 = (s32[1,1,64]{2,1,0:T(1,128)S(1)}, s32[1,1,64]{2,1,0:T(1,128)}, u32[]{:S(2)}) copy-start(s32[1,1,64]{2,1,0:T(1,128)} %param.7) | copy-start | bytes 772
  1.8 8.7 %collective-permute-start = (f32[264,128]{1,0:T(8,128)S(1)}, f32[264,128]{1,0:T(8,128)S(1)}, u32[]{:S(2)}, u32[]{:S(2)}) collective-permute-start(f32[264,128]{1,0:T(8,128)S(1)} %shard_map.46.refs_0_.refs_4_), channel_id=1, source_target_pairs={{0,4},{4,0},{8,12},{12,8},{16,20},{20,16},{24,28},{28,24},{1,5},{5... | collective-permute-start | bytes 405512 | tf_op jit(solution)/shard_map/ppermute | solution.py:26
  4.8 8.8 %collective-permute-start.1 = (f32[264,128]{1,0:T(8,128)S(1)}, f32[264,128]{1,0:T(8,128)S(1)}, u32[]{:S(2)}, u32[]{:S(2)}) collective-permute-start(f32[264,128]{1,0:T(8,128)S(1)} %shard_map.46.refs_0_.refs_4_), channel_id=1, source_target_pairs={{0,1},{1,0},{2,3},{3,2},{4,5},{5,4},{6,7},{7,6},{8,9},{9,8},{10,11... | collective-permute-start | bytes 405512 | tf_op jit(solution)/shard_map/ppermute | solution.py:26
  4.8 8.8 %collective-permute-start.4 = (f32[256,128]{1,0:T(8,128)}, f32[256,128]{1,0:T(8,128)S(1)}, u32[]{:S(2)}, u32[]{:S(2)}) collective-permute-start(f32[256,128]{1,0:T(8,128)} %bitcast.blocks), channel_id=1, source_target_pairs={{4,8},{8,4},{12,16},{16,12},{20,24},{24,20},{28,0},{0,28},{5,9},{9... | collective-permute-start | bytes 393224 | tf_op jit(solution)/shard_map/ppermute | solution.py:26
  8.4 6.9 %collective-permute-start.2 = (f32[264,128]{1,0:T(8,128)S(1)}, f32[264,128]{1,0:T(8,128)S(1)}, u32[]{:S(2)}, u32[]{:S(2)}) collective-permute-start(f32[264,128]{1,0:T(8,128)S(1)} %shard_map.46.refs_0_.refs_4_), channel_id=1, source_target_pairs={{1,2},{2,1},{3,0},{0,3},{5,6},{6,5},{7,4},{4,7},{9,10},{10,9},{11,... | collective-permute-start | bytes 405512 | tf_op jit(solution)/shard_map/ppermute | solution.py:26
  10.5 5.8 %collective-permute-start.3 = (f32[264,128]{1,0:T(8,128)S(1)}, f32[264,128]{1,0:T(8,128)S(1)}, u32[]{:S(2)}, u32[]{:S(2)}) collective-permute-start(f32[264,128]{1,0:T(8,128)S(1)} %collective-permute-done.refs_0_.refs_5_), channel_id=1, source_target_pairs={{0,1},{1,0},{2,3},{3,2},{4,5},{5,4},{6,7},{7,6},{8,9},{9,8},{10,11... | collective-permute-start | bytes 405512 | tf_op jit(solution)/shard_map/ppermute | solution.py:26
  10.8 6.1 %collective-permute-start.6 = (f32[264,128]{1,0:T(8,128)S(1)}, f32[264,128]{1,0:T(8,128)S(1)}, u32[]{:S(2)}, u32[]{:S(2)}) collective-permute-start(f32[264,128]{1,0:T(8,128)S(1)} %collective-permute-done.refs_0_.refs_5_), channel_id=1, source_target_pairs={{1,2},{2,1},{3,0},{0,3},{5,6},{6,5},{7,4},{4,7},{9,10},{10,9},{11,... | collective-permute-start | bytes 405512 | tf_op jit(solution)/shard_map/ppermute | solution.py:26
  13.6 2.7 %collective-permute-start.5 = (f32[256,128]{1,0:T(8,128)S(1)}, f32[256,128]{1,0:T(8,128)S(1)}, u32[]{:S(2)}, u32[]{:S(2)}) collective-permute-start(f32[256,128]{1,0:T(8,128)S(1)} %collective-permute-done.4.refs_1_), channel_id=1, source_target_pairs={{0,1},{1,0},{2,3},{3,2},{4,5},{5,4},{6,7},{7,6},{8,9},{9,8},{10,11... | collective-permute-start | bytes 393224 | tf_op jit(solution)/shard_map/ppermute | solution.py:26
  13.6 6.0 %collective-permute-start.7 = (f32[256,128]{1,0:T(8,128)S(1)}, f32[256,128]{1,0:T(8,128)S(1)}, u32[]{:S(2)}, u32[]{:S(2)}) collective-permute-start(f32[256,128]{1,0:T(8,128)S(1)} %collective-permute-done.4.refs_1_), channel_id=1, source_target_pairs={{1,2},{2,1},{3,0},{0,3},{5,6},{6,5},{7,4},{4,7},{9,10},{10,9},{11,... | collective-permute-start | bytes 393224 | tf_op jit(solution)/shard_map/ppermute | solution.py:26
  16.3 5.1 %copy-start = (s32[1,1,32,16]{2,3,1,0:T(8,128)S(1)}, s32[1,1,32,16]{2,3,1,0:T(8,128)}, u32[]{:S(2)}) copy-start(s32[1,1,32,16]{2,3,1,0:T(8,128)} %param.6) | copy-start | bytes 6148
  19.7 1.1 %collective-permute-start.8 = (f32[128]{0:T(128)S(1)}, f32[128]{0:T(128)S(1)}, u32[]{:S(2)}, u32[]{:S(2)}) collective-permute-start(f32[128]{0:T(128)S(1)} %get-tuple-element.32), channel_id=1, source_target_pairs={{0,1},{1,0},{2,3},{3,2},{4,5},{5,4},{6,7},{7,6},{8,9},{9,8},{10,11... | collective-permute-start | bytes 1544 | tf_op jit(solution)/shard_map/ppermute | solution.py:30
  20.8 3.9 %collective-permute-start.9 = (f32[128]{0:T(128)S(1)}, f32[128]{0:T(128)S(1)}, u32[]{:S(2)}, u32[]{:S(2)}) collective-permute-start(f32[128]{0:T(128)S(1)} %add_add_fusion.tie), channel_id=1, source_target_pairs={{0,8},{4,12},{8,0},{12,4},{16,24},{20,28},{24,16},{28,20},{1,9},{5... | collective-permute-start | bytes 1544 | tf_op jit(solution)/shard_map/ppermute | solution.py:30
  24.7 9.3 %collective-permute-start.10 = (f32[128]{0:T(128)S(1)}, f32[128]{0:T(128)S(1)}, u32[]{:S(2)}, u32[]{:S(2)}) collective-permute-start(f32[128]{0:T(128)S(1)} %add.11.tie.some_mass), channel_id=1, source_target_pairs={{0,16},{4,20},{8,24},{12,28},{16,0},{20,4},{24,8},{28,12},{1,17},{... | collective-permute-start | bytes 1544 | tf_op jit(solution)/shard_map/ppermute | solution.py:30
where the time goes:
time: 35.5 us; the launch traced here: 35.4 us
  Pallas kernels  16.8 us (47%)
  starting transfers between devices  13.3 us (37%)
  waiting for transfers between devices  3.88 us (11%)
  between operations  0.75 us (2%)
  local copies, waits for them, and re-layouts  0.66 us (2%)
    ppermute x8, starting transfers between devices, swap(): return lax.ppermute(block, axis, pairs)  11.2 us
    pallas_call x2, Pallas kernels, near_part(): pl.pallas_call(functools.partial(near_forces, places=places, count_blocks...  11.2 us
    ppermute x8, waiting for transfers between devices, swap(): return lax.ppermute(block, axis, pairs)  3.54 us
    ppermute x3, starting transfers between devices, exchange(): lax.ppermute(values, axis, [(i, i ^ step) for i in range(lax.axis_size(ax...  2.06 us
    pallas_call x1, Pallas kernels, body(): pl.pallas_call(functools.partial(add_far, half_gy=half_gy, total=total, u...  1.42 us
    pallas_call x1, Pallas kernels, body(): pl.pallas_call(functools.partial(last_rows, places=[(1, 1), (2, 0), (2, 1...  1.38 us
    pallas_call x1, Pallas kernels, body(): pl.pallas_call(functools.partial(mark, half_gy=half_gy), out_shape=jax.Sh...  1.15 us
    pallas_call x1, Pallas kernels, body(): pl.pallas_call(functools.partial(more_rows, places=[(1, 0), (0, 1), (0, 2...  1.03 us
  transfers between devices with their start and end apart: 11, of which 5 were waited for; matrix products, arithmetic and copies ran while one was open for 0% of the time, Pallas kernels for 40%

commit v1 on v0

--- a/solution.py
+++ b/solution.py
@@ -53,40 +53,58 @@
 
 
 def halves(low_half, pairs):
-    upper = [jnp.where(low_half, first, roll(second, 4)) for first, second in pairs]
-    lower = [jnp.where(low_half, roll(first, 4), second) for first, second in pairs]
-    return [jnp.concatenate(rows, axis=0).astype(BF16) for rows in (upper, lower)]
+    upper, lower = [], []
+    for (first, first_rolled), second in pairs:
+        second, second_rolled = second or (jnp.zeros_like(first),) * 2
+        upper.append(jnp.where(low_half, first, second_rolled))
+        lower.append(jnp.where(low_half, first_rolled, second))
+    return upper, lower
+
+
+def rows16(tiles):
+    return jnp.concatenate(tiles, axis=0).astype(BF16)
+
+
+def with_rolled(v):
+    return v, roll(v, 4)
+
+
+def masked(is_mass, value, pair):
+    return tuple(jnp.where(is_mass, value, v) for v in pair)
 
 
 def square_norm(is_mass, centred):
     square = jnp.where(is_mass, 0.0, centred)
     square = square * square
-    return (roll(square, 1) + roll(square, 2)) + roll(square, 3)
+    square = square + roll(square, 1)
+    return square + roll(square, 2)
 
 
 def source_tile(tile, moved, is_mass, low_half):
-    zero = jnp.zeros_like(tile)
     centred = (tile + moved) - jnp.where(is_mass, 0.0, middle)
     rows = jnp.where(is_mass, square_norm(is_mass, centred), -2.0 * centred)
-    high, mid, low = split3(rows)
-    high_1, mid_1 = jnp.where(is_mass, 1.0, high), jnp.where(is_mass, 1.0, mid)
-    features = halves(low_half, [(high, high_1), (high_1, mid), (mid_1, low), (zero, zero)])
+    high, mid, low = map(with_rolled, split3(rows))
+    high_1, mid_1 = masked(is_mass, 1.0, high), masked(is_mass, 1.0, mid)
+    features = halves(low_half, [(high, high_1), (high_1, mid), (mid_1, low)])
+    zero = jnp.zeros_like(tile)
     mass = jnp.where(is_mass, tile, 0.0)
-    mass = (mass + roll(mass, 7)) + (roll(mass, 6) + roll(mass, 5))
-    high, mid, low = split3(jnp.where(is_mass, 1.0, centred) * mass)
-    return features, halves(low_half, [(high, mid), (low, zero)])
+    mass = mass + roll(mass, 7)
+    mass = mass + roll(mass, 6)
+    high, mid, low = map(with_rolled, split3(jnp.where(is_mass, 1.0, centred) * mass))
+    moments = halves(low_half, [(high, mid), (low, None)])
+    return [rows16([*v, zero]) for v in features], [rows16(v) for v in moments]
 
 
 def target_tile(tile, is_mass, low_half):
-    zero = jnp.zeros_like(tile)
     centred = tile - middle
     norm = square_norm(is_mass, centred) + soft_near * soft_near
-    high, mid, low = split3(jnp.where(is_mass, norm, centred))
-    one_high = jnp.where(is_mass, 1.0, high)
-    high_mid = jnp.where(is_mass, high, mid)
-    mid_low = jnp.where(is_mass, mid, low)
-    low_mid = jnp.where(is_mass, low, mid)
-    return halves(low_half, [(one_high, high_mid), (mid_low, one_high), (low_mid, one_high), (zero, zero)])
+    high, mid, low = map(with_rolled, split3(jnp.where(is_mass, norm, centred)))
+    one_high = masked(is_mass, 1.0, high)
+    high_mid = tuple(jnp.where(is_mass, a, b) for a, b in zip(high, mid))
+    mid_low = tuple(jnp.where(is_mass, a, b) for a, b in zip(mid, low))
+    low_mid = tuple(jnp.where(is_mass, a, b) for a, b in zip(low, mid))
+    groups = halves(low_half, [(one_high, high_mid), (mid_low, one_high), (low_mid, one_high)])
+    return [rows16([*v, jnp.zeros_like(tile)]) for v in groups]
 
 
 def mark(blocks, ids_in, out, ids, sems, *, half_gy):
@@ -121,6 +139,7 @@
     is_mass, low_half = line % 4 == 3, line < 4
     is_x, is_y = line % 4 == 0, line % 4 == 1
     tiles = count_blocks // 2
+    unroll = math.gcd(tiles, 8)
     for piece, (row, col) in zip(pieces, places):
         a = (1, 2 * even_x, 2 - 2 * even_x)[row]
         b = (1, 2 * even_y, 2 - 2 * even_y)[col]
@@ -129,8 +148,8 @@
         moved = jnp.where(is_x, step_a, jnp.where(is_y, step_b, 0.0))
 
         def some_tiles(group, carry, piece=piece, base=(3 * a + b) * tiles, moved=moved):
-            for u in range(2):
-                at = group * 2 + u
+            for u in range(unroll):
+                at = group * unroll + u
                 tile = piece[pl.ds(pl.multiple_of(at * 8, 8), 8), :]
                 features, moments = source_tile(tile, moved, is_mass, low_half)
                 for half in range(2):
@@ -138,7 +157,7 @@
                     moment[2 * (base + at) + half] = moments[half]
             return carry
 
-        lax.fori_loop(0, tiles // 2, some_tiles, 0)
+        lax.fori_loop(0, tiles // unroll, some_tiles, 0)
 
 
 def start_rows(*refs, places, count_blocks):
@@ -201,35 +220,25 @@
                 out[c, pl.ds(at, 1), :] = sums[c : c + 1] - own * sums[3:4]
         return carry
 
-    groups = jnp.clip(limit[0, 0] - first + together - 1, 0, count) // together
+    groups = jnp.clip(limit - first + together - 1, 0, count) // together
     lax.fori_loop(0, groups, some_slots, 0)
 
 
-def near_forces(limit_in, lists_in, tie, feature_in, moment_in, target, centre, *refs, places, count_blocks, first, together):
-    pieces, (out, feature, moment, lists, limit, sems) = refs[:-6], refs[-6:]
-    copies = [pltpu.make_async_copy(lists_in, lists, sems.at[0]), pltpu.make_async_copy(limit_in, limit, sems.at[1])]
-    for copy in copies:
-        copy.start()
-    add_sources(pieces, places, feature, moment, count_blocks)
-    for copy in copies:
-        copy.wait()
+def near_forces(lists_in, tie, limit, feature, moment, target, centre, out, lists, sem, *, first, together):
+    copy = pltpu.make_async_copy(lists_in, lists, sem)
+    copy.start()
+    limit = jnp.max(limit[...].astype(F32)).astype(jnp.int32)
+    copy.wait()
     pair_sums(first, out.shape[1], limit, lists, feature, moment, target, centre, out, together)
 
 
-def add_far(limit_in, some_mass, more_mass, centre_in, *refs, half_gy, total, unroll):
-    nears, out, near, centre, masses, limit, sems = refs[:-6], *refs[-6:]
+def add_far(some_mass, more_mass, limit, centre, *refs, half_gy, total, unroll):
+    nears, out, masses, sems = refs[:-3], *refs[-3:]
     slots, width = out.shape[1:]
     copies = [
         pltpu.make_async_copy(some_mass, masses.at[0], sems.at[0]),
         pltpu.make_async_copy(more_mass, masses.at[1], sems.at[1]),
-        pltpu.make_async_copy(centre_in, centre, sems.at[2]),
-        pltpu.make_async_copy(limit_in, limit, sems.at[3]),
     ]
-    at = 0
-    for k, piece in enumerate(nears):
-        count = piece.shape[1]
-        copies.append(pltpu.make_async_copy(piece, near.at[:, pl.ds(at, count), :], sems.at[4 + k]))
-        at += count
     for copy in copies:
         copy.start()
     for copy in copies:
@@ -254,9 +263,10 @@
         return carry
 
     far = lax.fori_loop(0, total // unroll, cells, tuple(jnp.zeros_like(v) for v in position))
-    active = lax.broadcasted_iota(jnp.int32, (slots, width), 0) < limit[0, 0]
+    active = lax.broadcasted_iota(jnp.int32, (slots, width), 0) < limit[...]
     for c in range(3):
-        out[c] = jnp.where(active, near[c] + far[c], 0.0)
+        near = jnp.concatenate([piece[c] for piece in nears], axis=0)
+        out[c] = jnp.where(active, near + far[c], 0.0)
 
 
 def body(blocks, active_counts, pair_lists, cell_ids):
@@ -334,34 +344,32 @@
         **row_params,
     )(*table[:2], *more)
     table = [*rows_now, *table[2:]]
-    late, late_places = [second_xyy], [(2, 2)]
+    table[:2] = pl.pallas_call(
+        functools.partial(more_rows, places=[(2, 2)], count_blocks=count_blocks),
+        out_shape=table[:2],
+        in_specs=[vmem] * 3,
+        out_specs=[vmem] * 2,
+        input_output_aliases={0: 0, 1: 1},
+        compiler_params=row_params["compiler_params"],
+        cost_estimate=pl.CostEstimate(flops=5 * 10**9, bytes_accessed=1, transcendentals=0),
+    )(*table[:2], second_xyy)
 
     together = math.gcd(slots, 8)
     ranges = split_slots(slots, together)
 
-    def near_part(k, tie, table):
+    def near_part(k, tie):
         first, count = ranges[k]
-        pieces, places = (late, late_places) if k == 0 else ([], [])
-        near, *rows = pl.pallas_call(
-            functools.partial(
-                near_forces, places=places, count_blocks=count_blocks, first=first, together=math.gcd(count, 12 if count % 12 == 0 else 8)
-            ),
-            out_shape=[jax.ShapeDtypeStruct((3, count, width), F32), *table[:2]],
-            in_specs=[hbm] * 3 + [vmem] * (4 + len(pieces)),
-            out_specs=[vmem] * 3,
-            scratch_shapes=[
-                pltpu.SMEM((entries, slots), jnp.int32),
-                pltpu.SMEM((1, 1), jnp.int32),
-                pltpu.SemaphoreType.DMA((2,)),
-            ],
-            input_output_aliases={3: 1, 4: 2},
-            compiler_params=pltpu.CompilerParams(vmem_limit_bytes=24 * 2**20),
+        return pl.pallas_call(
+            functools.partial(near_forces, first=first, together=math.gcd(count, 24 if count % 24 == 0 else 8)),
+            out_shape=jax.ShapeDtypeStruct((3, count, width), F32),
+            in_specs=[hbm] * 2 + [vmem] * 5,
+            out_specs=vmem,
+            scratch_shapes=[pltpu.SMEM((entries, slots), jnp.int32), pltpu.SemaphoreType.DMA],
+            compiler_params=pltpu.CompilerParams(vmem_limit_bytes=16 * 2**20),
             cost_estimate=near_cost(count, entries, width),
-        )(active_counts, lists, tie, *table, *pieces)
-        return near, [*rows, *table[2:]]
+        )(lists, tie, active_counts, *table)
 
     if lax.axis_size("gy") == 4:
-        there_mass = lax.optimization_barrier((there_mass, second_xyy))[0]
         values = (here_mass + there_mass) + exchange(there_mass, "gy", 1)
         steps = []
     else:
@@ -370,32 +378,26 @@
     steps += [("gx", 2 << k) for k in range((lax.axis_size("gx") // 2).bit_length() - 1)]
     nears, parts = [], (values, jnp.zeros_like(values))
     for k, (axis, step) in enumerate(steps):
-        if nears:
-            values = lax.optimization_barrier((values, nears[-1]))[0]
+        values = lax.optimization_barrier((values, nears[-1] if nears else table[0]))[0]
         other = exchange(values, axis, step)
         parts = (values, other)
         if k >= len(steps) - 2 and len(nears) < len(ranges):
-            near, table = near_part(len(nears), values, table)
-            nears.append(near)
+            nears.append(near_part(len(nears), values))
         values = values + other
     while len(nears) < len(ranges):
-        near, table = near_part(len(nears), parts[0], table)
-        nears.append(near)
+        nears.append(near_part(len(nears), parts[0]))
 
     result = pl.pallas_call(
         functools.partial(add_far, half_gy=half_gy, total=total, unroll=math.gcd(total, 16)),
         out_shape=jax.ShapeDtypeStruct((3, slots, width), F32),
-        in_specs=[hbm] * (4 + len(nears)),
+        in_specs=[hbm] * 2 + [vmem] * (2 + len(nears)),
         out_specs=vmem,
         scratch_shapes=[
-            pltpu.VMEM((3, slots, width), F32),
-            pltpu.VMEM((3, slots, width), F32),
             pltpu.SMEM((2, lines * width), F32),
-            pltpu.SMEM((1, 1), jnp.int32),
-            pltpu.SemaphoreType.DMA((4 + len(nears),)),
+            pltpu.SemaphoreType.DMA((2,)),
         ],
         compiler_params=pltpu.CompilerParams(vmem_limit_bytes=4 * 2**20),
-    )(active_counts, *parts, table[3], *nears)
+    )(*parts, active_counts, table[3], *nears)
     return result.transpose(1, 0, 2)[None, None]
 
 

time: 35.5 us -> 34.2 us (0.963)
  the two profiles are of different devices: /device:TPU:0 before, /device:TPU:7 now
where the time goes in v1:
time: 34.2 us; the launch traced here: 34 us
  Pallas kernels  16 us (47%)
  starting transfers between devices  12.8 us (37%)
  waiting for transfers between devices  3.72 us (11%)
  between operations  0.76 us (2%)
  local copies, waits for them, and re-layouts  0.66 us (2%)
    pallas_call x2, Pallas kernels, near_part(): pl.pallas_call(functools.partial(near_forces, first=first, together=math....  10.8 us
    ppermute x8, starting transfers between devices, swap(): return lax.ppermute(block, axis, pairs)  10.1 us
    ppermute x8, waiting for transfers between devices, swap(): return lax.ppermute(block, axis, pairs)  3.62 us
    ppermute x3, starting transfers between devices, exchange(): lax.ppermute(values, axis, [(i, i ^ step) for i in range(lax.axis_size(ax...  2.77 us
    pallas_call x1, Pallas kernels, body(): pl.pallas_call(functools.partial(add_far, half_gy=half_gy, total=total, u...  1.32 us
    pallas_call x1, Pallas kernels, body(): pl.pallas_call(functools.partial(mark, half_gy=half_gy), out_shape=jax.Sh...  1.15 us
    pallas_call x1, Pallas kernels, body(): pl.pallas_call(functools.partial(last_rows, places=[(1, 1), (2, 0), (2, 1...  1.05 us
    pallas_call x1, Pallas kernels, body(): pl.pallas_call(functools.partial(more_rows, places=[(1, 0), (0, 1), (0, 2...  0.8 us
  transfers between devices with their start and end apart: 11, of which 4 were waited for; matrix products, arithmetic and copies ran while one was open for 0% of the time, Pallas kernels for 40%

profile of v1, /device:TPU:7, one launch (start us, length us, event | category | flops | bytes accessed | tf_op | source)
XLA Modules:
  0.0 34.0 jit_solution(17841927903985412209)
XLA Ops:
  0.0 0.7 %copy-done.1 = s32[1,1,64]{2,1,0:T(1,128)S(1)} copy-done((s32[1,1,64]{2,1,0:T(1,128)S(1)}, s32[1,1,64]{2,1,0:T(1,128)}, u32[]{:S(2)}) %copy-start.1) | copy-done | bytes 280
  0.7 1.2 %shard_map.46.refs_0_.refs_4_ = f32[264,128]{1,0:T(8,128)S(1)} custom-call(f32[256,128]{1,0:T(8,128)} %bitcast.blocks, s32[1,64]{1,0:T(1,128)S(1)} %bitcast.10), custom_call_target="tpu_custom_call" | custom-call | tf_op jit(solution)/shard_map/pallas_call | solution.py:284
  1.8 0.3 collective-permute-start
  2.1 1.0 %collective-permute-start.1 = (f32[264,128]{1,0:T(8,128)S(1)}, f32[264,128]{1,0:T(8,128)S(1)}, u32[]{:S(2)}, u32[]{:S(2)}) collective-permute-start(f32[264,128]{1,0:T(8,128)S(1)} %shard_map.46.refs_0_.refs_4_), channel_id=1, source_target_pairs={{0,1},{1,0},{2,3},{3,2},{4,5},{5,4},{6,7},{7,6},{8,9},{9,8},{10,11... | collective-permute-start | bytes 405512 | tf_op jit(solution)/shard_map/ppermute | solution.py:26
  3.1 2.2 %collective-permute-start.4 = (f32[256,128]{1,0:T(8,128)}, f32[256,128]{1,0:T(8,128)S(1)}, u32[]{:S(2)}, u32[]{:S(2)}) collective-permute-start(f32[256,128]{1,0:T(8,128)} %bitcast.blocks), channel_id=1, source_target_pairs={{4,8},{8,4},{12,16},{16,12},{20,24},{24,20},{28,0},{0,28},{5,9},{9... | collective-permute-start | bytes 393224 | tf_op jit(solution)/shard_map/ppermute | solution.py:26
  5.3 0.4 %collective-permute-start.2 = (f32[264,128]{1,0:T(8,128)S(1)}, f32[264,128]{1,0:T(8,128)S(1)}, u32[]{:S(2)}, u32[]{:S(2)}) collective-permute-start(f32[264,128]{1,0:T(8,128)S(1)} %shard_map.46.refs_0_.refs_4_), channel_id=1, source_target_pairs={{1,2},{2,1},{3,0},{0,3},{5,6},{6,5},{7,4},{4,7},{9,10},{10,9},{11,... | collective-permute-start | bytes 405512 | tf_op jit(solution)/shard_map/ppermute | solution.py:26
  5.7 0.6 %shard_map.47 = (bf16[576,32,128]{2,1,0:T(8,128)(2,1)S(1)}, bf16[576,16,128]{2,1,0:T(8,128)(2,1)S(1)}, bf16[32,32,128]{2,1,0:T(8,128)(2,1)S(1)}, f32[3,32,128]{2,1,0:T(8,128)S(1)}) custom-call(f32[264,128]{1,0:T(8,128)S(1)} %shard_map.46.refs_0_.refs_4_), custom_call_target="tpu_custom_call" | custom-call | flops 1 | bytes 1 | tf_op jit(solution)/shard_map/pallas_call | solution.py:302
  6.3 0.1 collective-permute-done.refs_0_.refs_5_
  6.3 4.4 %collective-permute-start.3 = (f32[264,128]{1,0:T(8,128)S(1)}, f32[264,128]{1,0:T(8,128)S(1)}, u32[]{:S(2)}, u32[]{:S(2)}) collective-permute-start(f32[264,128]{1,0:T(8,128)S(1)} %collective-permute-done.refs_0_.refs_5_), channel_id=1, source_target_pairs={{0,1},{1,0},{2,3},{3,2},{4,5},{5,4},{6,7},{7,6},{8,9},{9,8},{10,11... | collective-permute-start | bytes 405512 | tf_op jit(solution)/shard_map/ppermute | solution.py:26
  10.7 0.1 collective-permute-start.6
  10.8 0.0 collective-permute-done.4.refs_1_
  10.8 0.5 %collective-permute-start.5 = (f32[256,128]{1,0:T(8,128)S(1)}, f32[256,128]{1,0:T(8,128)S(1)}, u32[]{:S(2)}, u32[]{:S(2)}) collective-permute-start(f32[256,128]{1,0:T(8,128)S(1)} %collective-permute-done.4.refs_1_), channel_id=1, source_target_pairs={{0,1},{1,0},{2,3},{3,2},{4,5},{5,4},{6,7},{7,6},{8,9},{9,8},{10,11... | collective-permute-start | bytes 393224 | tf_op jit(solution)/shard_map/ppermute | solution.py:26
  11.3 0.0 collective-permute-done.1.refs_1_.refs_6_
  11.3 1.2 %collective-permute-start.8 = (f32[256,128]{1,0:T(8,128)S(1)}, f32[256,128]{1,0:T(8,128)S(1)}, u32[]{:S(2)}, u32[]{:S(2)}) collective-permute-start(f32[256,128]{1,0:T(8,128)S(1)} %collective-permute-done.4.refs_1_), channel_id=1, source_target_pairs={{1,2},{2,1},{3,0},{0,3},{5,6},{6,5},{7,4},{4,7},{9,10},{10,9},{11,... | collective-permute-start | bytes 393224 | tf_op jit(solution)/shard_map/ppermute | solution.py:26
  13.2 0.0 collective-permute-done.2.refs_2_.refs_7_
  13.2 0.8 %shard_map.48 = (bf16[576,32,128]{2,1,0:T(8,128)(2,1)S(1)}, bf16[576,16,128]{2,1,0:T(8,128)(2,1)S(1)}) custom-call(bf16[576,32,128]{2,1,0:T(8,128)(2,1)S(1)} %get-tuple-element.21.feature_in, bf16[576,16,128]{2,1,0:T(8,128)(2,1)S(1)} %get-tuple-element.22.moment_in, ...), custom_call_target="tpu_custom_call", output_to_operand_aliasing={{0}: (0, {}), {1}: (1, {})} | custom-call | flops 1 | bytes 1 | tf_op jit(solution)/shard_map/pallas_call | solution.py:320
  14.0 0.0 collective-permute-done.5.refs_2_
  14.0 0.0 collective-permute-done.3.refs_0_
  14.0 2.8 %collective-permute-done.6.refs_3_ = f32[264,128]{1,0:T(8,128)S(1)} collective-permute-done((f32[264,128]{1,0:T(8,128)S(1)}, f32[264,128]{1,0:T(8,128)S(1)}, u32[]{:S(2)}, u32[]{:S(2)}) %collective-permute-start.6) | collective-permute-done | bytes 135200 | tf_op jit(solution)/shard_map/ppermute | solution.py:26
  16.8 1.0 %shard_map.49 = (bf16[576,32,128]{2,1,0:T(8,128)(2,1)S(1)}, bf16[576,16,128]{2,1,0:T(8,128)(2,1)S(1)}, f32[128]{0:T(128)S(1)}, f32[128]{0:T(128)S(1)}) custom-call(bf16[576,32,128]{2,1,0:T(8,128)(2,1)S(1)} %get-tuple-element.25.feature_in, bf16[576,16,128]{2,1,0:T(8,128)(2,1)S(1)} %get-tuple-element.26.moment_in, ...), custom_call_target="tpu_custom_call", output_to_operand_aliasing={{0}: (0, {}), {1}: (1, {})} | custom-call | flops 1 | bytes 1 | tf_op jit(solution)/shard_map/pallas_call | solution.py:332
  17.9 0.1 collective-permute-start.7
  18.0 0.7 %collective-permute-done.8.refs_0_ = f32[256,128]{1,0:T(8,128)S(1)} collective-permute-done((f32[256,128]{1,0:T(8,128)S(1)}, f32[256,128]{1,0:T(8,128)S(1)}, u32[]{:S(2)}, u32[]{:S(2)}) %collective-permute-start.8) | collective-permute-done | bytes 131104 | tf_op jit(solution)/shard_map/ppermute | solution.py:26
  18.7 0.3 shard_map.50
  19.0 0.1 collective-permute-done.7
  19.1 1.3 %collective-permute-start.9 = (f32[128]{0:T(128)S(1)}, f32[128]{0:T(128)S(1)}, u32[]{:S(2)}, u32[]{:S(2)}) collective-permute-start(f32[128]{0:T(128)S(1)} %add_add_fusion.tie), channel_id=1, source_target_pairs={{0,8},{4,12},{8,0},{12,4},{16,24},{20,28},{24,16},{28,20},{1,9},{5... | collective-permute-start | bytes 1544 | tf_op jit(solution)/shard_map/ppermute | solution.py:30
  20.4 0.0 copy-done
  20.4 3.2 %shard_map.51.refs_0_ = f32[3,8,128]{2,1,0:T(8,128)S(1)} custom-call(s32[16,32]{1,0:T(8,128)S(1)} %bitcast.8, f32[128]{0:T(128)S(1)} %add_add_fusion.tie, s32[1,1]{1,0:T(1,128)S(6)} %copy.17.limit, bf16[576,32,128]{2,1,0:T(8,128)(2,1)S(1)} %get-tuple-element.32.feature, bf16[576,16,128]{2,1,0:T(8,128)(2,1)S(1)} %get-tuple-element.34.moment, ...), custom_call_target="tpu_custom_call" | custom-call | flops 41943040 | bytes 12288 | tf_op jit(solution)/shard_map/pallas_call | solution.py:362
  23.6 0.0 collective-permute-done.9
  23.6 1.4 %collective-permute-start.10 = (f32[128]{0:T(128)S(1)}, f32[128]{0:T(128)S(1)}, u32[]{:S(2)}, u32[]{:S(2)}) collective-permute-start(f32[128]{0:T(128)S(1)} %add.11.tie.some_mass), channel_id=1, source_target_pairs={{0,16},{4,20},{8,24},{12,28},{16,0},{20,4},{24,8},{28,12},{1,17},{... | collective-permute-start | bytes 1544 | tf_op jit(solution)/shard_map/ppermute | solution.py:30
  25.0 7.6 %shard_map.52.refs_1_ = f32[3,24,128]{2,1,0:T(8,128)S(1)} custom-call(s32[16,32]{1,0:T(8,128)S(1)} %bitcast.9, f32[128]{0:T(128)S(1)} %add.11.tie.some_mass, s32[1,1]{1,0:T(1,128)S(6)} %copy.17.limit, bf16[576,32,128]{2,1,0:T(8,128)(2,1)S(1)} %get-tuple-element.32.feature, bf16[576,16,128]{2,1,0:T(8,128)(2,1)S(1)} %get-tuple-element.34.moment, ...), custom_call_target="tpu_custom_call" | custom-call | flops 125829120 | bytes 36864 | tf_op jit(solution)/shard_map/pallas_call | solution.py:362
  32.6 0.0 collective-permute-done.10.more_mass
  32.6 1.3 %shard_map.53 = f32[3,32,128]{2,1,0:T(8,128)} custom-call(f32[128]{0:T(128)S(1)} %add.11.tie.some_mass, f32[128]{0:T(128)S(1)} %collective-permute-done.10.more_mass, s32[1,1]{1,0:T(1,128)S(6)} %copy.17.limit, f32[3,32,128]{2,1,0:T(8,128)S(1)} %get-tuple-element.23.centre, f32[3,8,128]{2,1,0:T(8,128)S(1)} %shard_map.51.refs_0_, ...), custom_call_target="tpu_custom_call" | custom-call | tf_op jit(solution)/shard_map/pallas_call | solution.py:390
  (4 shorter events, 0.0 us)
Async XLA Ops:
  0.0 0.7 %copy-start.1 = (s32[1,1,64]{2,1,0:T(1,128)S(1)}, s32[1,1,64]{2,1,0:T(1,128)}, u32[]{:S(2)}) copy-start(s32[1,1,64]{2,1,0:T(1,128)} %param.7) | copy-start | bytes 772
  1.8 4.5 %collective-permute-start = (f32[264,128]{1,0:T(8,128)S(1)}, f32[264,128]{1,0:T(8,128)S(1)}, u32[]{:S(2)}, u32[]{:S(2)}) collective-permute-start(f32[264,128]{1,0:T(8,128)S(1)} %shard_map.46.refs_0_.refs_4_), channel_id=1, source_target_pairs={{0,4},{4,0},{8,12},{12,8},{16,20},{20,16},{24,28},{28,24},{1,5},{5... | collective-permute-start | bytes 405512 | tf_op jit(solution)/shard_map/ppermute | solution.py:26
  2.1 9.2 %collective-permute-start.1 = (f32[264,128]{1,0:T(8,128)S(1)}, f32[264,128]{1,0:T(8,128)S(1)}, u32[]{:S(2)}, u32[]{:S(2)}) collective-permute-start(f32[264,128]{1,0:T(8,128)S(1)} %shard_map.46.refs_0_.refs_4_), channel_id=1, source_target_pairs={{0,1},{1,0},{2,3},{3,2},{4,5},{5,4},{6,7},{7,6},{8,9},{9,8},{10,11... | collective-permute-start | bytes 405512 | tf_op jit(solution)/shard_map/ppermute | solution.py:26
  3.1 7.7 %collective-permute-start.4 = (f32[256,128]{1,0:T(8,128)}, f32[256,128]{1,0:T(8,128)S(1)}, u32[]{:S(2)}, u32[]{:S(2)}) collective-permute-start(f32[256,128]{1,0:T(8,128)} %bitcast.blocks), channel_id=1, source_target_pairs={{4,8},{8,4},{12,16},{16,12},{20,24},{24,20},{28,0},{0,28},{5,9},{9... | collective-permute-start | bytes 393224 | tf_op jit(solution)/shard_map/ppermute | solution.py:26
  5.3 7.9 %collective-permute-start.2 = (f32[264,128]{1,0:T(8,128)S(1)}, f32[264,128]{1,0:T(8,128)S(1)}, u32[]{:S(2)}, u32[]{:S(2)}) collective-permute-start(f32[264,128]{1,0:T(8,128)S(1)} %shard_map.46.refs_0_.refs_4_), channel_id=1, source_target_pairs={{1,2},{2,1},{3,0},{0,3},{5,6},{6,5},{7,4},{4,7},{9,10},{10,9},{11,... | collective-permute-start | bytes 405512 | tf_op jit(solution)/shard_map/ppermute | solution.py:26
  6.3 7.7 %collective-permute-start.3 = (f32[264,128]{1,0:T(8,128)S(1)}, f32[264,128]{1,0:T(8,128)S(1)}, u32[]{:S(2)}, u32[]{:S(2)}) collective-permute-start(f32[264,128]{1,0:T(8,128)S(1)} %collective-permute-done.refs_0_.refs_5_), channel_id=1, source_target_pairs={{0,1},{1,0},{2,3},{3,2},{4,5},{5,4},{6,7},{7,6},{8,9},{9,8},{10,11... | collective-permute-start | bytes 405512 | tf_op jit(solution)/shard_map/ppermute | solution.py:26
  10.7 6.1 %collective-permute-start.6 = (f32[264,128]{1,0:T(8,128)S(1)}, f32[264,128]{1,0:T(8,128)S(1)}, u32[]{:S(2)}, u32[]{:S(2)}) collective-permute-start(f32[264,128]{1,0:T(8,128)S(1)} %collective-permute-done.refs_0_.refs_5_), channel_id=1, source_target_pairs={{1,2},{2,1},{3,0},{0,3},{5,6},{6,5},{7,4},{4,7},{9,10},{10,9},{11,... | collective-permute-start | bytes 405512 | tf_op jit(solution)/shard_map/ppermute | solution.py:26
  10.8 3.2 %collective-permute-start.5 = (f32[256,128]{1,0:T(8,128)S(1)}, f32[256,128]{1,0:T(8,128)S(1)}, u32[]{:S(2)}, u32[]{:S(2)}) collective-permute-start(f32[256,128]{1,0:T(8,128)S(1)} %collective-permute-done.4.refs_1_), channel_id=1, source_target_pairs={{0,1},{1,0},{2,3},{3,2},{4,5},{5,4},{6,7},{7,6},{8,9},{9,8},{10,11... | collective-permute-start | bytes 393224 | tf_op jit(solution)/shard_map/ppermute | solution.py:26
  11.3 7.4 %collective-permute-start.8 = (f32[256,128]{1,0:T(8,128)S(1)}, f32[256,128]{1,0:T(8,128)S(1)}, u32[]{:S(2)}, u32[]{:S(2)}) collective-permute-start(f32[256,128]{1,0:T(8,128)S(1)} %collective-permute-done.4.refs_1_), channel_id=1, source_target_pairs={{1,2},{2,1},{3,0},{0,3},{5,6},{6,5},{7,4},{4,7},{9,10},{10,9},{11,... | collective-permute-start | bytes 393224 | tf_op jit(solution)/shard_map/ppermute | solution.py:26
  17.9 1.2 %collective-permute-start.7 = (f32[128]{0:T(128)S(1)}, f32[128]{0:T(128)S(1)}, u32[]{:S(2)}, u32[]{:S(2)}) collective-permute-start(f32[128]{0:T(128)S(1)} %get-tuple-element.29), channel_id=1, source_target_pairs={{0,1},{1,0},{2,3},{3,2},{4,5},{5,4},{6,7},{7,6},{8,9},{9,8},{10,11... | collective-permute-start | bytes 1544 | tf_op jit(solution)/shard_map/ppermute | solution.py:30
  18.7 1.7 %copy-start = (s32[1,1,32,16]{2,3,1,0:T(8,128)S(1)}, s32[1,1,32,16]{2,3,1,0:T(8,128)}, u32[]{:S(2)}) copy-start(s32[1,1,32,16]{2,3,1,0:T(8,128)} %param.6) | copy-start | bytes 6148
  19.1 4.5 %collective-permute-start.9 = (f32[128]{0:T(128)S(1)}, f32[128]{0:T(128)S(1)}, u32[]{:S(2)}, u32[]{:S(2)}) collective-permute-start(f32[128]{0:T(128)S(1)} %add_add_fusion.tie), channel_id=1, source_target_pairs={{0,8},{4,12},{8,0},{12,4},{16,24},{20,28},{24,16},{28,20},{1,9},{5... | collective-permute-start | bytes 1544 | tf_op jit(solution)/shard_map/ppermute | solution.py:30
  23.6 9.0 %collective-permute-start.10 = (f32[128]{0:T(128)S(1)}, f32[128]{0:T(128)S(1)}, u32[]{:S(2)}, u32[]{:S(2)}) collective-permute-start(f32[128]{0:T(128)S(1)} %add.11.tie.some_mass), channel_id=1, source_target_pairs={{0,16},{4,20},{8,24},{12,28},{16,0},{20,4},{24,8},{28,12},{1,17},{... | collective-permute-start | bytes 1544 | tf_op jit(solution)/shard_map/ppermute | solution.py:30

commit v2 on v1

--- a/solution.py
+++ b/solution.py
@@ -232,37 +232,24 @@
     pair_sums(first, out.shape[1], limit, lists, feature, moment, target, centre, out, together)
 
 
-def add_far(some_mass, more_mass, limit, centre, *refs, half_gy, total, unroll):
-    nears, out, masses, sems = refs[:-3], *refs[-3:]
+def add_far(some_mass, more_mass, limit, centre, *refs, half_gy, total):
+    nears, out = refs[:-1], refs[-1]
     slots, width = out.shape[1:]
-    copies = [
-        pltpu.make_async_copy(some_mass, masses.at[0], sems.at[0]),
-        pltpu.make_async_copy(more_mass, masses.at[1], sems.at[1]),
-    ]
-    for copy in copies:
-        copy.start()
-    for copy in copies:
-        copy.wait()
     corner = (lax.axis_index("gx").astype(F32) + middle, lax.axis_index("gy").astype(F32) + middle, middle)
     position = [centre[c] + corner[c] for c in range(3)]
-
-    def cells(step, carry):
-        for u in range(unroll):
-            cell = step * unroll + u
-            group, sub_cell = cell // SUBC, cell % SUBC
-            centre = (
-                (2 * (group // half_gy) + 1).astype(F32),
-                (2 * (group % half_gy) + 1).astype(F32),
-                (sub_cell.astype(F32) + 0.5) * (1.0 / SUBC),
-            )
-            offset = [centre[c] - position[c] for c in range(3)]
+    far = [jnp.zeros((slots, width), F32)] * 3
+    for line in range(-(-total // width)):
+        at = pl.ds(line * width, width)
+        masses = (some_mass[at] + more_mass[at]).reshape(1, width)
+        for cell in range(line * width, min(total, (line + 1) * width)):
+            group, sub_cell = divmod(cell, SUBC)
+            middle_of = (2.0 * (group // half_gy) + 1, 2.0 * (group % half_gy) + 1, (sub_cell + 0.5) / SUBC)
+            offset = [middle_of[c] - position[c] for c in range(3)]
             dist_sq = (offset[0] * offset[0] + offset[1] * offset[1]) + offset[2] * offset[2]
             inverse = lax.rsqrt(dist_sq + soft_far * soft_far)
-            weight = (masses[0, cell] + masses[1, cell]) * (inverse * inverse * inverse)
-            carry = tuple(carry[c] + weight * offset[c] for c in range(3))
-        return carry
-
-    far = lax.fori_loop(0, total // unroll, cells, tuple(jnp.zeros_like(v) for v in position))
+            lane = cell - line * width
+            weight = masses[:, lane : lane + 1] * (inverse * inverse * inverse)
+            far = [far[c] + weight * offset[c] for c in range(3)]
     active = lax.broadcasted_iota(jnp.int32, (slots, width), 0) < limit[...]
     for c in range(3):
         near = jnp.concatenate([piece[c] for piece in nears], axis=0)
@@ -388,15 +375,11 @@
         nears.append(near_part(len(nears), parts[0]))
 
     result = pl.pallas_call(
-        functools.partial(add_far, half_gy=half_gy, total=total, unroll=math.gcd(total, 16)),
+        functools.partial(add_far, half_gy=half_gy, total=total),
         out_shape=jax.ShapeDtypeStruct((3, slots, width), F32),
-        in_specs=[hbm] * 2 + [vmem] * (2 + len(nears)),
+        in_specs=[vmem] * (4 + len(nears)),
         out_specs=vmem,
-        scratch_shapes=[
-            pltpu.SMEM((2, lines * width), F32),
-            pltpu.SemaphoreType.DMA((2,)),
-        ],
-        compiler_params=pltpu.CompilerParams(vmem_limit_bytes=4 * 2**20),
+        compiler_params=pltpu.CompilerParams(vmem_limit_bytes=12 * 2**20),
     )(*parts, active_counts, table[3], *nears)
     return result.transpose(1, 0, 2)[None, None]
 

time: 34.2 us -> 33.8 us (0.988)
  the two profiles are of different devices: /device:TPU:7 before, /device:TPU:0 now
where the time goes in v2:
time: 33.8 us; the launch traced here: 33.6 us
  Pallas kernels  15.4 us (46%)
  starting transfers between devices  14.1 us (42%)
  waiting for transfers between devices  2.72 us (8%)
  between operations  0.77 us (2%)
  local copies, waits for them, and re-layouts  0.66 us (2%)
    ppermute x8, starting transfers between devices, swap(): return lax.ppermute(block, axis, pairs)  11.2 us
    pallas_call x2, Pallas kernels, near_part(): pl.pallas_call(functools.partial(near_forces, first=first, together=math....  10.8 us
    ppermute x3, starting transfers between devices, exchange(): lax.ppermute(values, axis, [(i, i ^ step) for i in range(lax.axis_size(ax...  2.87 us
    ppermute x8, waiting for transfers between devices, swap(): return lax.ppermute(block, axis, pairs)  2.71 us
    pallas_call x1, Pallas kernels, body(): pl.pallas_call(functools.partial(mark, half_gy=half_gy), out_shape=jax.Sh...  1.15 us
    pallas_call x1, Pallas kernels, body(): pl.pallas_call(functools.partial(last_rows, places=[(1, 1), (2, 0), (2, 1...  1.05 us
    pallas_call x1, Pallas kernels, body(): pl.pallas_call(functools.partial(more_rows, places=[(1, 0), (0, 1), (0, 2...  0.8 us
    pallas_call x1, Pallas kernels, body(): pl.pallas_call(functools.partial(add_far, half_gy=half_gy, total=total),...  0.76 us
  transfers between devices with their start and end apart: 11, of which 4 were waited for; matrix products, arithmetic and copies ran while one was open for 0% of the time, Pallas kernels for 40%

profile of v2, /device:TPU:0, one launch (start us, length us, event | category | flops | bytes accessed | tf_op | source)
XLA Modules:
  0.0 33.6 jit_solution(17368129371260535531)
XLA Ops:
  0.0 0.7 %copy-done.1 = s32[1,1,64]{2,1,0:T(1,128)S(1)} copy-done((s32[1,1,64]{2,1,0:T(1,128)S(1)}, s32[1,1,64]{2,1,0:T(1,128)}, u32[]{:S(2)}) %copy-start.1) | copy-done | bytes 280
  0.7 1.2 %shard_map.46.refs_0_.refs_4_ = f32[264,128]{1,0:T(8,128)S(1)} custom-call(f32[256,128]{1,0:T(8,128)} %bitcast.blocks, s32[1,64]{1,0:T(1,128)S(1)} %bitcast.10), custom_call_target="tpu_custom_call" | custom-call | tf_op jit(solution)/shard_map/pallas_call | solution.py:271
  1.8 3.0 %collective-permute-start = (f32[264,128]{1,0:T(8,128)S(1)}, f32[264,128]{1,0:T(8,128)S(1)}, u32[]{:S(2)}, u32[]{:S(2)}) collective-permute-start(f32[264,128]{1,0:T(8,128)S(1)} %shard_map.46.refs_0_.refs_4_), channel_id=1, source_target_pairs={{0,4},{4,0},{8,12},{12,8},{16,20},{20,16},{24,28},{28,24},{1,5},{5... | collective-permute-start | bytes 405512 | tf_op jit(solution)/shard_map/ppermute | solution.py:26
  4.8 0.0 collective-permute-start.1
  4.8 3.6 %collective-permute-start.4 = (f32[256,128]{1,0:T(8,128)}, f32[256,128]{1,0:T(8,128)S(1)}, u32[]{:S(2)}, u32[]{:S(2)}) collective-permute-start(f32[256,128]{1,0:T(8,128)} %bitcast.blocks), channel_id=1, source_target_pairs={{4,8},{8,4},{12,16},{16,12},{20,24},{24,20},{28,0},{0,28},{5,9},{9... | collective-permute-start | bytes 393224 | tf_op jit(solution)/shard_map/ppermute | solution.py:26
  8.4 1.4 %collective-permute-start.2 = (f32[264,128]{1,0:T(8,128)S(1)}, f32[264,128]{1,0:T(8,128)S(1)}, u32[]{:S(2)}, u32[]{:S(2)}) collective-permute-start(f32[264,128]{1,0:T(8,128)S(1)} %shard_map.46.refs_0_.refs_4_), channel_id=1, source_target_pairs={{1,2},{2,1},{3,0},{0,3},{5,6},{6,5},{7,4},{4,7},{9,10},{10,9},{11,... | collective-permute-start | bytes 405512 | tf_op jit(solution)/shard_map/ppermute | solution.py:26
  9.7 0.6 %shard_map.47 = (bf16[576,32,128]{2,1,0:T(8,128)(2,1)S(1)}, bf16[576,16,128]{2,1,0:T(8,128)(2,1)S(1)}, bf16[32,32,128]{2,1,0:T(8,128)(2,1)S(1)}, f32[3,32,128]{2,1,0:T(8,128)S(1)}) custom-call(f32[264,128]{1,0:T(8,128)S(1)} %shard_map.46.refs_0_.refs_4_), custom_call_target="tpu_custom_call" | custom-call | flops 1 | bytes 1 | tf_op jit(solution)/shard_map/pallas_call | solution.py:289
  10.3 0.2 collective-permute-done.refs_0_.refs_5_
  10.5 0.2 collective-permute-start.3
  10.7 1.5 %collective-permute-start.6 = (f32[264,128]{1,0:T(8,128)S(1)}, f32[264,128]{1,0:T(8,128)S(1)}, u32[]{:S(2)}, u32[]{:S(2)}) collective-permute-start(f32[264,128]{1,0:T(8,128)S(1)} %collective-permute-done.refs_0_.refs_5_), channel_id=1, source_target_pairs={{1,2},{2,1},{3,0},{0,3},{5,6},{6,5},{7,4},{4,7},{9,10},{10,9},{11,... | collective-permute-start | bytes 405512 | tf_op jit(solution)/shard_map/ppermute | solution.py:26
  12.1 1.5 %collective-permute-done.4.refs_1_ = f32[256,128]{1,0:T(8,128)S(1)} collective-permute-done((f32[256,128]{1,0:T(8,128)}, f32[256,128]{1,0:T(8,128)S(1)}, u32[]{:S(2)}, u32[]{:S(2)}) %collective-permute-start.4) | collective-permute-done | bytes 131104 | tf_op jit(solution)/shard_map/ppermute | solution.py:26
  13.6 0.0 collective-permute-start.5
  13.6 0.0 collective-permute-done.1.refs_1_.refs_6_
  13.6 1.6 %collective-permute-start.8 = (f32[256,128]{1,0:T(8,128)S(1)}, f32[256,128]{1,0:T(8,128)S(1)}, u32[]{:S(2)}, u32[]{:S(2)}) collective-permute-start(f32[256,128]{1,0:T(8,128)S(1)} %collective-permute-done.4.refs_1_), channel_id=1, source_target_pairs={{1,2},{2,1},{3,0},{0,3},{5,6},{6,5},{7,4},{4,7},{9,10},{10,9},{11,... | collective-permute-start | bytes 393224 | tf_op jit(solution)/shard_map/ppermute | solution.py:26
  15.9 0.0 collective-permute-done.2.refs_2_.refs_7_
  15.9 0.8 %shard_map.48 = (bf16[576,32,128]{2,1,0:T(8,128)(2,1)S(1)}, bf16[576,16,128]{2,1,0:T(8,128)(2,1)S(1)}) custom-call(bf16[576,32,128]{2,1,0:T(8,128)(2,1)S(1)} %get-tuple-element.21.feature_in, bf16[576,16,128]{2,1,0:T(8,128)(2,1)S(1)} %get-tuple-element.22.moment_in, ...), custom_call_target="tpu_custom_call", output_to_operand_aliasing={{0}: (0, {}), {1}: (1, {})} | custom-call | flops 1 | bytes 1 | tf_op jit(solution)/shard_map/pallas_call | solution.py:307
  16.8 0.0 collective-permute-done.5.refs_2_
  16.8 0.0 collective-permute-done.3.refs_0_
  16.8 0.1 collective-permute-done.6.refs_3_
  16.9 1.0 %shard_map.49 = (bf16[576,32,128]{2,1,0:T(8,128)(2,1)S(1)}, bf16[576,16,128]{2,1,0:T(8,128)(2,1)S(1)}, f32[128]{0:T(128)S(1)}, f32[128]{0:T(128)S(1)}) custom-call(bf16[576,32,128]{2,1,0:T(8,128)(2,1)S(1)} %get-tuple-element.25.feature_in, bf16[576,16,128]{2,1,0:T(8,128)(2,1)S(1)} %get-tuple-element.26.moment_in, ...), custom_call_target="tpu_custom_call", output_to_operand_aliasing={{0}: (0, {}), {1}: (1, {})} | custom-call | flops 1 | bytes 1 | tf_op jit(solution)/shard_map/pallas_call | solution.py:319
  17.9 0.8 %collective-permute-start.7 = (f32[128]{0:T(128)S(1)}, f32[128]{0:T(128)S(1)}, u32[]{:S(2)}, u32[]{:S(2)}) collective-permute-start(f32[128]{0:T(128)S(1)} %get-tuple-element.29), channel_id=1, source_target_pairs={{0,1},{1,0},{2,3},{3,2},{4,5},{5,4},{6,7},{7,6},{8,9},{9,8},{10,11... | collective-permute-start | bytes 1544 | tf_op jit(solution)/shard_map/ppermute | solution.py:30
  18.7 0.9 %collective-permute-done.8.refs_0_ = f32[256,128]{1,0:T(8,128)S(1)} collective-permute-done((f32[256,128]{1,0:T(8,128)S(1)}, f32[256,128]{1,0:T(8,128)S(1)}, u32[]{:S(2)}, u32[]{:S(2)}) %collective-permute-start.8) | collective-permute-done | bytes 131104 | tf_op jit(solution)/shard_map/ppermute | solution.py:26
  19.7 0.3 shard_map.50
  19.9 0.0 collective-permute-done.7
  20.0 0.7 %collective-permute-start.9 = (f32[128]{0:T(128)S(1)}, f32[128]{0:T(128)S(1)}, u32[]{:S(2)}, u32[]{:S(2)}) collective-permute-start(f32[128]{0:T(128)S(1)} %add_add_fusion.tie), channel_id=1, source_target_pairs={{0,8},{4,12},{8,0},{12,4},{16,24},{20,28},{24,16},{28,20},{1,9},{5... | collective-permute-start | bytes 1544 | tf_op jit(solution)/shard_map/ppermute | solution.py:30
  20.7 0.0 copy-done
  20.7 3.2 %shard_map.51.refs_0_ = f32[3,8,128]{2,1,0:T(8,128)S(1)} custom-call(s32[16,32]{1,0:T(8,128)S(1)} %bitcast.8, f32[128]{0:T(128)S(1)} %add_add_fusion.tie, s32[1,1]{1,0:T(1,128)S(6)} %copy.17.limit, bf16[576,32,128]{2,1,0:T(8,128)(2,1)S(1)} %get-tuple-element.32.feature, bf16[576,16,128]{2,1,0:T(8,128)(2,1)S(1)} %get-tuple-element.34.moment, ...), custom_call_target="tpu_custom_call" | custom-call | flops 41943040 | bytes 12288 | tf_op jit(solution)/shard_map/pallas_call | solution.py:349
  23.9 0.0 collective-permute-done.9
  23.9 1.3 %collective-permute-start.10 = (f32[128]{0:T(128)S(1)}, f32[128]{0:T(128)S(1)}, u32[]{:S(2)}, u32[]{:S(2)}) collective-permute-start(f32[128]{0:T(128)S(1)} %add.11.tie.some_mass), channel_id=1, source_target_pairs={{0,16},{4,20},{8,24},{12,28},{16,0},{20,4},{24,8},{28,12},{1,17},{... | collective-permute-start | bytes 1544 | tf_op jit(solution)/shard_map/ppermute | solution.py:30
  25.3 7.6 %shard_map.52.refs_1_ = f32[3,24,128]{2,1,0:T(8,128)S(1)} custom-call(s32[16,32]{1,0:T(8,128)S(1)} %bitcast.9, f32[128]{0:T(128)S(1)} %add.11.tie.some_mass, s32[1,1]{1,0:T(1,128)S(6)} %copy.17.limit, bf16[576,32,128]{2,1,0:T(8,128)(2,1)S(1)} %get-tuple-element.32.feature, bf16[576,16,128]{2,1,0:T(8,128)(2,1)S(1)} %get-tuple-element.34.moment, ...), custom_call_target="tpu_custom_call" | custom-call | flops 125829120 | bytes 36864 | tf_op jit(solution)/shard_map/pallas_call | solution.py:349
  32.9 0.0 collective-permute-done.10.more_mass
  32.9 0.8 %shard_map.53 = f32[3,32,128]{2,1,0:T(8,128)} custom-call(f32[128]{0:T(128)S(1)} %add.11.tie.some_mass, f32[128]{0:T(128)S(1)} %collective-permute-done.10.more_mass, s32[1,1]{1,0:T(1,128)S(6)} %copy.17.limit, f32[3,32,128]{2,1,0:T(8,128)S(1)} %get-tuple-element.23.centre, f32[3,8,128]{2,1,0:T(8,128)S(1)} %shard_map.51.refs_0_, ...), custom_call_target="tpu_custom_call" | custom-call | tf_op jit(solution)/shard_map/pallas_call | solution.py:377
  (4 shorter events, 0.0 us)
Async XLA Ops:
  0.0 0.7 %copy-start.1 = (s32[1,1,64]{2,1,0:T(1,128)S(1)}, s32[1,1,64]{2,1,0:T(1,128)}, u32[]{:S(2)}) copy-start(s32[1,1,64]{2,1,0:T(1,128)} %param.7) | copy-start | bytes 772
  1.8 8.7 %collective-permute-start = (f32[264,128]{1,0:T(8,128)S(1)}, f32[264,128]{1,0:T(8,128)S(1)}, u32[]{:S(2)}, u32[]{:S(2)}) collective-permute-start(f32[264,128]{1,0:T(8,128)S(1)} %shard_map.46.refs_0_.refs_4_), channel_id=1, source_target_pairs={{0,4},{4,0},{8,12},{12,8},{16,20},{20,16},{24,28},{28,24},{1,5},{5... | collective-permute-start | bytes 405512 | tf_op jit(solution)/shard_map/ppermute | solution.py:26
  4.8 8.8 %collective-permute-start.1 = (f32[264,128]{1,0:T(8,128)S(1)}, f32[264,128]{1,0:T(8,128)S(1)}, u32[]{:S(2)}, u32[]{:S(2)}) collective-permute-start(f32[264,128]{1,0:T(8,128)S(1)} %shard_map.46.refs_0_.refs_4_), channel_id=1, source_target_pairs={{0,1},{1,0},{2,3},{3,2},{4,5},{5,4},{6,7},{7,6},{8,9},{9,8},{10,11... | collective-permute-start | bytes 405512 | tf_op jit(solution)/shard_map/ppermute | solution.py:26
  4.8 8.8 %collective-permute-start.4 = (f32[256,128]{1,0:T(8,128)}, f32[256,128]{1,0:T(8,128)S(1)}, u32[]{:S(2)}, u32[]{:S(2)}) collective-permute-start(f32[256,128]{1,0:T(8,128)} %bitcast.blocks), channel_id=1, source_target_pairs={{4,8},{8,4},{12,16},{16,12},{20,24},{24,20},{28,0},{0,28},{5,9},{9... | collective-permute-start | bytes 393224 | tf_op jit(solution)/shard_map/ppermute | solution.py:26
  8.4 7.5 %collective-permute-start.2 = (f32[264,128]{1,0:T(8,128)S(1)}, f32[264,128]{1,0:T(8,128)S(1)}, u32[]{:S(2)}, u32[]{:S(2)}) collective-permute-start(f32[264,128]{1,0:T(8,128)S(1)} %shard_map.46.refs_0_.refs_4_), channel_id=1, source_target_pairs={{1,2},{2,1},{3,0},{0,3},{5,6},{6,5},{7,4},{4,7},{9,10},{10,9},{11,... | collective-permute-start | bytes 405512 | tf_op jit(solution)/shard_map/ppermute | solution.py:26
  10.5 6.3 %collective-permute-start.3 = (f32[264,128]{1,0:T(8,128)S(1)}, f32[264,128]{1,0:T(8,128)S(1)}, u32[]{:S(2)}, u32[]{:S(2)}) collective-permute-start(f32[264,128]{1,0:T(8,128)S(1)} %collective-permute-done.refs_0_.refs_5_), channel_id=1, source_target_pairs={{0,1},{1,0},{2,3},{3,2},{4,5},{5,4},{6,7},{7,6},{8,9},{9,8},{10,11... | collective-permute-start | bytes 405512 | tf_op jit(solution)/shard_map/ppermute | solution.py:26
  10.7 6.2 %collective-permute-start.6 = (f32[264,128]{1,0:T(8,128)S(1)}, f32[264,128]{1,0:T(8,128)S(1)}, u32[]{:S(2)}, u32[]{:S(2)}) collective-permute-start(f32[264,128]{1,0:T(8,128)S(1)} %collective-permute-done.refs_0_.refs_5_), channel_id=1, source_target_pairs={{1,2},{2,1},{3,0},{0,3},{5,6},{6,5},{7,4},{4,7},{9,10},{10,9},{11,... | collective-permute-start | bytes 405512 | tf_op jit(solution)/shard_map/ppermute | solution.py:26
  13.6 3.1 %collective-permute-start.5 = (f32[256,128]{1,0:T(8,128)S(1)}, f32[256,128]{1,0:T(8,128)S(1)}, u32[]{:S(2)}, u32[]{:S(2)}) collective-permute-start(f32[256,128]{1,0:T(8,128)S(1)} %collective-permute-done.4.refs_1_), channel_id=1, source_target_pairs={{0,1},{1,0},{2,3},{3,2},{4,5},{5,4},{6,7},{7,6},{8,9},{9,8},{10,11... | collective-permute-start | bytes 393224 | tf_op jit(solution)/shard_map/ppermute | solution.py:26
  13.6 6.0 %collective-permute-start.8 = (f32[256,128]{1,0:T(8,128)S(1)}, f32[256,128]{1,0:T(8,128)S(1)}, u32[]{:S(2)}, u32[]{:S(2)}) collective-permute-start(f32[256,128]{1,0:T(8,128)S(1)} %collective-permute-done.4.refs_1_), channel_id=1, source_target_pairs={{1,2},{2,1},{3,0},{0,3},{5,6},{6,5},{7,4},{4,7},{9,10},{10,9},{11,... | collective-permute-start | bytes 393224 | tf_op jit(solution)/shard_map/ppermute | solution.py:26
  17.9 2.0 %collective-permute-start.7 = (f32[128]{0:T(128)S(1)}, f32[128]{0:T(128)S(1)}, u32[]{:S(2)}, u32[]{:S(2)}) collective-permute-start(f32[128]{0:T(128)S(1)} %get-tuple-element.29), channel_id=1, source_target_pairs={{0,1},{1,0},{2,3},{3,2},{4,5},{5,4},{6,7},{7,6},{8,9},{9,8},{10,11... | collective-permute-start | bytes 1544 | tf_op jit(solution)/shard_map/ppermute | solution.py:30
  19.7 1.0 %copy-start = (s32[1,1,32,16]{2,3,1,0:T(8,128)S(1)}, s32[1,1,32,16]{2,3,1,0:T(8,128)}, u32[]{:S(2)}) copy-start(s32[1,1,32,16]{2,3,1,0:T(8,128)} %param.6) | copy-start | bytes 6148
  20.0 3.9 %collective-permute-start.9 = (f32[128]{0:T(128)S(1)}, f32[128]{0:T(128)S(1)}, u32[]{:S(2)}, u32[]{:S(2)}) collective-permute-start(f32[128]{0:T(128)S(1)} %add_add_fusion.tie), channel_id=1, source_target_pairs={{0,8},{4,12},{8,0},{12,4},{16,24},{20,28},{24,16},{28,20},{1,9},{5... | collective-permute-start | bytes 1544 | tf_op jit(solution)/shard_map/ppermute | solution.py:30
  23.9 8.9 %collective-permute-start.10 = (f32[128]{0:T(128)S(1)}, f32[128]{0:T(128)S(1)}, u32[]{:S(2)}, u32[]{:S(2)}) collective-permute-start(f32[128]{0:T(128)S(1)} %add.11.tie.some_mass), channel_id=1, source_target_pairs={{0,16},{4,20},{8,24},{12,28},{16,0},{20,4},{24,8},{28,12},{1,17},{... | collective-permute-start | bytes 1544 | tf_op jit(solution)/shard_map/ppermute | solution.py:30

commit v3 on v2

--- a/solution.py
+++ b/solution.py
@@ -32,7 +32,7 @@
 
 def split_slots(slots, together):
     groups = slots // together
-    cuts = [0, max(1, groups // 4), groups]
+    cuts = [0, max(1, groups // 2), groups]
     return [(a * together, (b - a) * together) for a, b in zip(cuts, cuts[1:]) if b > a]
 
 
@@ -347,7 +347,7 @@
     def near_part(k, tie):
         first, count = ranges[k]
         return pl.pallas_call(
-            functools.partial(near_forces, first=first, together=math.gcd(count, 24 if count % 24 == 0 else 8)),
+            functools.partial(near_forces, first=first, together=math.gcd(count, 16)),
             out_shape=jax.ShapeDtypeStruct((3, count, width), F32),
             in_specs=[hbm] * 2 + [vmem] * 5,
             out_specs=vmem,

time: 33.8 us -> 33.7 us (level)
  no operation moved by 1% of the time
where the time goes in v3:
time: 33.7 us; the launch traced here: 33.5 us
  Pallas kernels  15.4 us (46%)
  starting transfers between devices  14 us (42%)
  waiting for transfers between devices  2.72 us (8%)
  between operations  0.77 us (2%)
  local copies, waits for them, and re-layouts  0.66 us (2%)
    ppermute x8, starting transfers between devices, swap(): return lax.ppermute(block, axis, pairs)  11.2 us
    pallas_call x2, Pallas kernels, near_part(): pl.pallas_call(functools.partial(near_forces, first=first, together=math....  10.8 us
    ppermute x3, starting transfers between devices, exchange(): lax.ppermute(values, axis, [(i, i ^ step) for i in range(lax.axis_size(ax...  2.76 us
    ppermute x8, waiting for transfers between devices, swap(): return lax.ppermute(block, axis, pairs)  2.71 us
    pallas_call x1, Pallas kernels, body(): pl.pallas_call(functools.partial(mark, half_gy=half_gy), out_shape=jax.Sh...  1.15 us
    pallas_call x1, Pallas kernels, body(): pl.pallas_call(functools.partial(last_rows, places=[(1, 1), (2, 0), (2, 1...  1.05 us
    pallas_call x1, Pallas kernels, body(): pl.pallas_call(functools.partial(more_rows, places=[(1, 0), (0, 1), (0, 2...  0.8 us
    pallas_call x1, Pallas kernels, body(): pl.pallas_call(functools.partial(add_far, half_gy=half_gy, total=total),...  0.76 us
  transfers between devices with their start and end apart: 11, of which 4 were waited for; matrix products, arithmetic and copies ran while one was open for 0% of the time, Pallas kernels for 40%

profile of v3, /device:TPU:0, one launch (start us, length us, event | category | flops | bytes accessed | tf_op | source)
XLA Modules:
  0.0 33.5 jit_solution(16166438597760238415)
XLA Ops:
  0.0 0.7 %copy-done = s32[1,1,64]{2,1,0:T(1,128)S(1)} copy-done((s32[1,1,64]{2,1,0:T(1,128)S(1)}, s32[1,1,64]{2,1,0:T(1,128)}, u32[]{:S(2)}) %copy-start) | copy-done | bytes 280
  0.7 1.2 %shard_map.46.refs_0_.refs_4_ = f32[264,128]{1,0:T(8,128)S(1)} custom-call(f32[256,128]{1,0:T(8,128)} %bitcast.blocks, s32[1,64]{1,0:T(1,128)S(1)} %bitcast.8), custom_call_target="tpu_custom_call" | custom-call | tf_op jit(solution)/shard_map/pallas_call | solution.py:271
  1.8 3.0 %collective-permute-start = (f32[264,128]{1,0:T(8,128)S(1)}, f32[264,128]{1,0:T(8,128)S(1)}, u32[]{:S(2)}, u32[]{:S(2)}) collective-permute-start(f32[264,128]{1,0:T(8,128)S(1)} %shard_map.46.refs_0_.refs_4_), channel_id=1, source_target_pairs={{0,4},{4,0},{8,12},{12,8},{16,20},{20,16},{24,28},{28,24},{1,5},{5... | collective-permute-start | bytes 405512 | tf_op jit(solution)/shard_map/ppermute | solution.py:26
  4.8 0.0 collective-permute-start.1
  4.8 3.6 %collective-permute-start.4 = (f32[256,128]{1,0:T(8,128)}, f32[256,128]{1,0:T(8,128)S(1)}, u32[]{:S(2)}, u32[]{:S(2)}) collective-permute-start(f32[256,128]{1,0:T(8,128)} %bitcast.blocks), channel_id=1, source_target_pairs={{4,8},{8,4},{12,16},{16,12},{20,24},{24,20},{28,0},{0,28},{5,9},{9... | collective-permute-start | bytes 393224 | tf_op jit(solution)/shard_map/ppermute | solution.py:26
  8.4 1.4 %collective-permute-start.2 = (f32[264,128]{1,0:T(8,128)S(1)}, f32[264,128]{1,0:T(8,128)S(1)}, u32[]{:S(2)}, u32[]{:S(2)}) collective-permute-start(f32[264,128]{1,0:T(8,128)S(1)} %shard_map.46.refs_0_.refs_4_), channel_id=1, source_target_pairs={{1,2},{2,1},{3,0},{0,3},{5,6},{6,5},{7,4},{4,7},{9,10},{10,9},{11,... | collective-permute-start | bytes 405512 | tf_op jit(solution)/shard_map/ppermute | solution.py:26
  9.7 0.6 %shard_map.47 = (bf16[576,32,128]{2,1,0:T(8,128)(2,1)S(1)}, bf16[576,16,128]{2,1,0:T(8,128)(2,1)S(1)}, bf16[32,32,128]{2,1,0:T(8,128)(2,1)S(1)}, f32[3,32,128]{2,1,0:T(8,128)S(1)}) custom-call(f32[264,128]{1,0:T(8,128)S(1)} %shard_map.46.refs_0_.refs_4_), custom_call_target="tpu_custom_call" | custom-call | flops 1 | bytes 1 | tf_op jit(solution)/shard_map/pallas_call | solution.py:289
  10.3 0.2 collective-permute-done.refs_0_.refs_5_
  10.5 0.2 collective-permute-start.3
  10.7 1.5 %collective-permute-start.6 = (f32[264,128]{1,0:T(8,128)S(1)}, f32[264,128]{1,0:T(8,128)S(1)}, u32[]{:S(2)}, u32[]{:S(2)}) collective-permute-start(f32[264,128]{1,0:T(8,128)S(1)} %collective-permute-done.refs_0_.refs_5_), channel_id=1, source_target_pairs={{1,2},{2,1},{3,0},{0,3},{5,6},{6,5},{7,4},{4,7},{9,10},{10,9},{11,... | collective-permute-start | bytes 405512 | tf_op jit(solution)/shard_map/ppermute | solution.py:26
  12.1 1.5 %collective-permute-done.4.refs_1_ = f32[256,128]{1,0:T(8,128)S(1)} collective-permute-done((f32[256,128]{1,0:T(8,128)}, f32[256,128]{1,0:T(8,128)S(1)}, u32[]{:S(2)}, u32[]{:S(2)}) %collective-permute-start.4) | collective-permute-done | bytes 131104 | tf_op jit(solution)/shard_map/ppermute | solution.py:26
  13.6 0.0 collective-permute-start.5
  13.6 0.0 collective-permute-done.1.refs_1_.refs_6_
  13.6 1.6 %collective-permute-start.8 = (f32[256,128]{1,0:T(8,128)S(1)}, f32[256,128]{1,0:T(8,128)S(1)}, u32[]{:S(2)}, u32[]{:S(2)}) collective-permute-start(f32[256,128]{1,0:T(8,128)S(1)} %collective-permute-done.4.refs_1_), channel_id=1, source_target_pairs={{1,2},{2,1},{3,0},{0,3},{5,6},{6,5},{7,4},{4,7},{9,10},{10,9},{11,... | collective-permute-start | bytes 393224 | tf_op jit(solution)/shard_map/ppermute | solution.py:26
  15.9 0.0 collective-permute-done.2.refs_2_.refs_7_
  15.9 0.8 %shard_map.48 = (bf16[576,32,128]{2,1,0:T(8,128)(2,1)S(1)}, bf16[576,16,128]{2,1,0:T(8,128)(2,1)S(1)}) custom-call(bf16[576,32,128]{2,1,0:T(8,128)(2,1)S(1)} %get-tuple-element.21.feature_in, bf16[576,16,128]{2,1,0:T(8,128)(2,1)S(1)} %get-tuple-element.22.moment_in, ...), custom_call_target="tpu_custom_call", output_to_operand_aliasing={{0}: (0, {}), {1}: (1, {})} | custom-call | flops 1 | bytes 1 | tf_op jit(solution)/shard_map/pallas_call | solution.py:307
  16.8 0.0 collective-permute-done.5.refs_2_
  16.8 0.0 collective-permute-done.3.refs_0_
  16.8 0.1 collective-permute-done.6.refs_3_
  16.9 1.0 %shard_map.49 = (bf16[576,32,128]{2,1,0:T(8,128)(2,1)S(1)}, bf16[576,16,128]{2,1,0:T(8,128)(2,1)S(1)}, f32[128]{0:T(128)S(1)}, f32[128]{0:T(128)S(1)}) custom-call(bf16[576,32,128]{2,1,0:T(8,128)(2,1)S(1)} %get-tuple-element.25.feature_in, bf16[576,16,128]{2,1,0:T(8,128)(2,1)S(1)} %get-tuple-element.26.moment_in, ...), custom_call_target="tpu_custom_call", output_to_operand_aliasing={{0}: (0, {}), {1}: (1, {})} | custom-call | flops 1 | bytes 1 | tf_op jit(solution)/shard_map/pallas_call | solution.py:319
  17.9 0.8 %collective-permute-start.7 = (f32[128]{0:T(128)S(1)}, f32[128]{0:T(128)S(1)}, u32[]{:S(2)}, u32[]{:S(2)}) collective-permute-start(f32[128]{0:T(128)S(1)} %get-tuple-element.29), channel_id=1, source_target_pairs={{0,1},{1,0},{2,3},{3,2},{4,5},{5,4},{6,7},{7,6},{8,9},{9,8},{10,11... | collective-permute-start | bytes 1544 | tf_op jit(solution)/shard_map/ppermute | solution.py:30
  18.7 0.9 %collective-permute-done.8.refs_0_ = f32[256,128]{1,0:T(8,128)S(1)} collective-permute-done((f32[256,128]{1,0:T(8,128)S(1)}, f32[256,128]{1,0:T(8,128)S(1)}, u32[]{:S(2)}, u32[]{:S(2)}) %collective-permute-start.8) | collective-permute-done | bytes 131104 | tf_op jit(solution)/shard_map/ppermute | solution.py:26
  19.7 0.3 shard_map.50
  19.9 0.0 collective-permute-done.7
  20.0 0.7 %collective-permute-start.9 = (f32[128]{0:T(128)S(1)}, f32[128]{0:T(128)S(1)}, u32[]{:S(2)}, u32[]{:S(2)}) collective-permute-start(f32[128]{0:T(128)S(1)} %add_add_fusion.tie), channel_id=1, source_target_pairs={{0,8},{4,12},{8,0},{12,4},{16,24},{20,28},{24,16},{28,20},{1,9},{5... | collective-permute-start | bytes 1544 | tf_op jit(solution)/shard_map/ppermute | solution.py:30
  20.7 0.0 copy-done.1
  20.7 5.4 %shard_map.51.refs_0_ = f32[3,16,128]{2,1,0:T(8,128)S(1)} custom-call(s32[16,32]{1,0:T(8,128)S(1)} %bitcast.9, f32[128]{0:T(128)S(1)} %add_add_fusion.tie, s32[1,1]{1,0:T(1,128)S(6)} %copy.17.limit, bf16[576,32,128]{2,1,0:T(8,128)(2,1)S(1)} %get-tuple-element.32.feature, bf16[576,16,128]{2,1,0:T(8,128)(2,1)S(1)} %get-tuple-element.34.moment, ...), custom_call_target="tpu_custom_call" | custom-call | flops 83886080 | bytes 24576 | tf_op jit(solution)/shard_map/pallas_call | solution.py:349
  26.1 0.0 collective-permute-done.9
  26.1 1.2 %collective-permute-start.10 = (f32[128]{0:T(128)S(1)}, f32[128]{0:T(128)S(1)}, u32[]{:S(2)}, u32[]{:S(2)}) collective-permute-start(f32[128]{0:T(128)S(1)} %add.11.tie.some_mass), channel_id=1, source_target_pairs={{0,16},{4,20},{8,24},{12,28},{16,0},{20,4},{24,8},{28,12},{1,17},{... | collective-permute-start | bytes 1544 | tf_op jit(solution)/shard_map/ppermute | solution.py:30
  27.3 5.4 %shard_map.52.refs_1_ = f32[3,16,128]{2,1,0:T(8,128)S(1)} custom-call(s32[16,32]{1,0:T(8,128)S(1)} %bitcast.10, f32[128]{0:T(128)S(1)} %add.11.tie.some_mass, s32[1,1]{1,0:T(1,128)S(6)} %copy.17.limit, bf16[576,32,128]{2,1,0:T(8,128)(2,1)S(1)} %get-tuple-element.32.feature, bf16[576,16,128]{2,1,0:T(8,128)(2,1)S(1)} %get-tuple-element.34.moment, ...), custom_call_target="tpu_custom_call" | custom-call | flops 83886080 | bytes 24576 | tf_op jit(solution)/shard_map/pallas_call | solution.py:349
  32.8 0.0 collective-permute-done.10.more_mass
  32.8 0.8 %shard_map.53 = f32[3,32,128]{2,1,0:T(8,128)} custom-call(f32[128]{0:T(128)S(1)} %add.11.tie.some_mass, f32[128]{0:T(128)S(1)} %collective-permute-done.10.more_mass, s32[1,1]{1,0:T(1,128)S(6)} %copy.17.limit, f32[3,32,128]{2,1,0:T(8,128)S(1)} %get-tuple-element.23.centre, f32[3,16,128]{2,1,0:T(8,128)S(1)} %shard_map.51.refs_0_, ...), custom_call_target="tpu_custom_call" | custom-call | tf_op jit(solution)/shard_map/pallas_call | solution.py:377
  (4 shorter events, 0.0 us)
Async XLA Ops:
  0.0 0.7 %copy-start = (s32[1,1,64]{2,1,0:T(1,128)S(1)}, s32[1,1,64]{2,1,0:T(1,128)}, u32[]{:S(2)}) copy-start(s32[1,1,64]{2,1,0:T(1,128)} %param.7) | copy-start | bytes 772
  1.8 8.7 %collective-permute-start = (f32[264,128]{1,0:T(8,128)S(1)}, f32[264,128]{1,0:T(8,128)S(1)}, u32[]{:S(2)}, u32[]{:S(2)}) collective-permute-start(f32[264,128]{1,0:T(8,128)S(1)} %shard_map.46.refs_0_.refs_4_), channel_id=1, source_target_pairs={{0,4},{4,0},{8,12},{12,8},{16,20},{20,16},{24,28},{28,24},{1,5},{5... | collective-permute-start | bytes 405512 | tf_op jit(solution)/shard_map/ppermute | solution.py:26
  4.8 8.8 %collective-permute-start.1 = (f32[264,128]{1,0:T(8,128)S(1)}, f32[264,128]{1,0:T(8,128)S(1)}, u32[]{:S(2)}, u32[]{:S(2)}) collective-permute-start(f32[264,128]{1,0:T(8,128)S(1)} %shard_map.46.refs_0_.refs_4_), channel_id=1, source_target_pairs={{0,1},{1,0},{2,3},{3,2},{4,5},{5,4},{6,7},{7,6},{8,9},{9,8},{10,11... | collective-permute-start | bytes 405512 | tf_op jit(solution)/shard_map/ppermute | solution.py:26
  4.8 8.8 %collective-permute-start.4 = (f32[256,128]{1,0:T(8,128)}, f32[256,128]{1,0:T(8,128)S(1)}, u32[]{:S(2)}, u32[]{:S(2)}) collective-permute-start(f32[256,128]{1,0:T(8,128)} %bitcast.blocks), channel_id=1, source_target_pairs={{4,8},{8,4},{12,16},{16,12},{20,24},{24,20},{28,0},{0,28},{5,9},{9... | collective-permute-start | bytes 393224 | tf_op jit(solution)/shard_map/ppermute | solution.py:26
  8.4 7.5 %collective-permute-start.2 = (f32[264,128]{1,0:T(8,128)S(1)}, f32[264,128]{1,0:T(8,128)S(1)}, u32[]{:S(2)}, u32[]{:S(2)}) collective-permute-start(f32[264,128]{1,0:T(8,128)S(1)} %shard_map.46.refs_0_.refs_4_), channel_id=1, source_target_pairs={{1,2},{2,1},{3,0},{0,3},{5,6},{6,5},{7,4},{4,7},{9,10},{10,9},{11,... | collective-permute-start | bytes 405512 | tf_op jit(solution)/shard_map/ppermute | solution.py:26
  10.5 6.3 %collective-permute-start.3 = (f32[264,128]{1,0:T(8,128)S(1)}, f32[264,128]{1,0:T(8,128)S(1)}, u32[]{:S(2)}, u32[]{:S(2)}) collective-permute-start(f32[264,128]{1,0:T(8,128)S(1)} %collective-permute-done.refs_0_.refs_5_), channel_id=1, source_target_pairs={{0,1},{1,0},{2,3},{3,2},{4,5},{5,4},{6,7},{7,6},{8,9},{9,8},{10,11... | collective-permute-start | bytes 405512 | tf_op jit(solution)/shard_map/ppermute | solution.py:26
  10.7 6.2 %collective-permute-start.6 = (f32[264,128]{1,0:T(8,128)S(1)}, f32[264,128]{1,0:T(8,128)S(1)}, u32[]{:S(2)}, u32[]{:S(2)}) collective-permute-start(f32[264,128]{1,0:T(8,128)S(1)} %collective-permute-done.refs_0_.refs_5_), channel_id=1, source_target_pairs={{1,2},{2,1},{3,0},{0,3},{5,6},{6,5},{7,4},{4,7},{9,10},{10,9},{11,... | collective-permute-start | bytes 405512 | tf_op jit(solution)/shard_map/ppermute | solution.py:26
  13.6 3.1 %collective-permute-start.5 = (f32[256,128]{1,0:T(8,128)S(1)}, f32[256,128]{1,0:T(8,128)S(1)}, u32[]{:S(2)}, u32[]{:S(2)}) collective-permute-start(f32[256,128]{1,0:T(8,128)S(1)} %collective-permute-done.4.refs_1_), channel_id=1, source_target_pairs={{0,1},{1,0},{2,3},{3,2},{4,5},{5,4},{6,7},{7,6},{8,9},{9,8},{10,11... | collective-permute-start | bytes 393224 | tf_op jit(solution)/shard_map/ppermute | solution.py:26
  13.6 6.0 %collective-permute-start.8 = (f32[256,128]{1,0:T(8,128)S(1)}, f32[256,128]{1,0:T(8,128)S(1)}, u32[]{:S(2)}, u32[]{:S(2)}) collective-permute-start(f32[256,128]{1,0:T(8,128)S(1)} %collective-permute-done.4.refs_1_), channel_id=1, source_target_pairs={{1,2},{2,1},{3,0},{0,3},{5,6},{6,5},{7,4},{4,7},{9,10},{10,9},{11,... | collective-permute-start | bytes 393224 | tf_op jit(solution)/shard_map/ppermute | solution.py:26
  17.9 2.0 %collective-permute-start.7 = (f32[128]{0:T(128)S(1)}, f32[128]{0:T(128)S(1)}, u32[]{:S(2)}, u32[]{:S(2)}) collective-permute-start(f32[128]{0:T(128)S(1)} %get-tuple-element.29), channel_id=1, source_target_pairs={{0,1},{1,0},{2,3},{3,2},{4,5},{5,4},{6,7},{7,6},{8,9},{9,8},{10,11... | collective-permute-start | bytes 1544 | tf_op jit(solution)/shard_map/ppermute | solution.py:30
  19.7 1.0 %copy-start.1 = (s32[1,1,32,16]{2,3,1,0:T(8,128)S(1)}, s32[1,1,32,16]{2,3,1,0:T(8,128)}, u32[]{:S(2)}) copy-start(s32[1,1,32,16]{2,3,1,0:T(8,128)} %param.6) | copy-start | bytes 6148
  20.0 6.1 %collective-permute-start.9 = (f32[128]{0:T(128)S(1)}, f32[128]{0:T(128)S(1)}, u32[]{:S(2)}, u32[]{:S(2)}) collective-permute-start(f32[128]{0:T(128)S(1)} %add_add_fusion.tie), channel_id=1, source_target_pairs={{0,8},{4,12},{8,0},{12,4},{16,24},{20,28},{24,16},{28,20},{1,9},{5... | collective-permute-start | bytes 1544 | tf_op jit(solution)/shard_map/ppermute | solution.py:30
  26.1 6.6 %collective-permute-start.10 = (f32[128]{0:T(128)S(1)}, f32[128]{0:T(128)S(1)}, u32[]{:S(2)}, u32[]{:S(2)}) collective-permute-start(f32[128]{0:T(128)S(1)} %add.11.tie.some_mass), channel_id=1, source_target_pairs={{0,16},{4,20},{8,24},{12,28},{16,0},{20,4},{24,8},{28,12},{1,17},{... | collective-permute-start | bytes 1544 | tf_op jit(solution)/shard_map/ppermute | solution.py:30

commit v4 on v3

--- a/solution.py
+++ b/solution.py
@@ -139,7 +139,7 @@
     is_mass, low_half = line % 4 == 3, line < 4
     is_x, is_y = line % 4 == 0, line % 4 == 1
     tiles = count_blocks // 2
-    unroll = math.gcd(tiles, 8)
+    unroll = math.gcd(tiles, 16)
     for piece, (row, col) in zip(pieces, places):
         a = (1, 2 * even_x, 2 - 2 * even_x)[row]
         b = (1, 2 * even_y, 2 - 2 * even_y)[col]

time: 33.7 us -> 33.6 us (level)
  the two profiles are of different devices: /device:TPU:0 before, /device:TPU:3 now
where the time goes in v4:
time: 33.6 us; the launch traced here: 33.4 us
  Pallas kernels  15.3 us (46%)
  starting transfers between devices  12.9 us (38%)
  waiting for transfers between devices  3.72 us (11%)
  between operations  0.78 us (2%)
  local copies, waits for them, and re-layouts  0.66 us (2%)
    pallas_call x2, Pallas kernels, near_part(): pl.pallas_call(functools.partial(near_forces, first=first, together=math....  10.8 us
    ppermute x8, starting transfers between devices, swap(): return lax.ppermute(block, axis, pairs)  10.1 us
    ppermute x8, waiting for transfers between devices, swap(): return lax.ppermute(block, axis, pairs)  3.66 us
    ppermute x3, starting transfers between devices, exchange(): lax.ppermute(values, axis, [(i, i ^ step) for i in range(lax.axis_size(ax...  2.81 us
    pallas_call x1, Pallas kernels, body(): pl.pallas_call(functools.partial(mark, half_gy=half_gy), out_shape=jax.Sh...  1.15 us
    pallas_call x1, Pallas kernels, body(): pl.pallas_call(functools.partial(last_rows, places=[(1, 1), (2, 0), (2, 1...  1 us
    pallas_call x1, Pallas kernels, body(): pl.pallas_call(functools.partial(more_rows, places=[(1, 0), (0, 1), (0, 2...  0.77 us
    pallas_call x1, Pallas kernels, body(): pl.pallas_call(functools.partial(add_far, half_gy=half_gy, total=total),...  0.76 us
  transfers between devices with their start and end apart: 11, of which 3 were waited for; matrix products, arithmetic and copies ran while one was open for 0% of the time, Pallas kernels for 40%

profile of v4, /device:TPU:3, one launch (start us, length us, event | category | flops | bytes accessed | tf_op | source)
XLA Modules:
  0.0 33.4 jit_solution(15722335200111971760)
XLA Ops:
  0.0 0.7 %copy-done = s32[1,1,64]{2,1,0:T(1,128)S(1)} copy-done((s32[1,1,64]{2,1,0:T(1,128)S(1)}, s32[1,1,64]{2,1,0:T(1,128)}, u32[]{:S(2)}) %copy-start) | copy-done | bytes 280
  0.7 1.2 %shard_map.46.refs_0_.refs_4_ = f32[264,128]{1,0:T(8,128)S(1)} custom-call(f32[256,128]{1,0:T(8,128)} %bitcast.blocks, s32[1,64]{1,0:T(1,128)S(1)} %bitcast.8), custom_call_target="tpu_custom_call" | custom-call | tf_op jit(solution)/shard_map/pallas_call | solution.py:271
  1.8 0.1 collective-permute-start
  1.9 0.7 %collective-permute-start.1 = (f32[264,128]{1,0:T(8,128)S(1)}, f32[264,128]{1,0:T(8,128)S(1)}, u32[]{:S(2)}, u32[]{:S(2)}) collective-permute-start(f32[264,128]{1,0:T(8,128)S(1)} %shard_map.46.refs_0_.refs_4_), channel_id=1, source_target_pairs={{0,1},{1,0},{2,3},{3,2},{4,5},{5,4},{6,7},{7,6},{8,9},{9,8},{10,11... | collective-permute-start | bytes 405512 | tf_op jit(solution)/shard_map/ppermute | solution.py:26
  2.6 2.7 %collective-permute-start.4 = (f32[256,128]{1,0:T(8,128)}, f32[256,128]{1,0:T(8,128)S(1)}, u32[]{:S(2)}, u32[]{:S(2)}) collective-permute-start(f32[256,128]{1,0:T(8,128)} %bitcast.blocks), channel_id=1, source_target_pairs={{4,8},{8,4},{12,16},{16,12},{20,24},{24,20},{28,0},{0,28},{5,9},{9... | collective-permute-start | bytes 393224 | tf_op jit(solution)/shard_map/ppermute | solution.py:26
  5.3 1.4 %collective-permute-start.2 = (f32[264,128]{1,0:T(8,128)S(1)}, f32[264,128]{1,0:T(8,128)S(1)}, u32[]{:S(2)}, u32[]{:S(2)}) collective-permute-start(f32[264,128]{1,0:T(8,128)S(1)} %shard_map.46.refs_0_.refs_4_), channel_id=1, source_target_pairs={{1,2},{2,1},{3,0},{0,3},{5,6},{6,5},{7,4},{4,7},{9,10},{10,9},{11,... | collective-permute-start | bytes 405512 | tf_op jit(solution)/shard_map/ppermute | solution.py:26
  6.7 0.6 %shard_map.47 = (bf16[576,32,128]{2,1,0:T(8,128)(2,1)S(1)}, bf16[576,16,128]{2,1,0:T(8,128)(2,1)S(1)}, bf16[32,32,128]{2,1,0:T(8,128)(2,1)S(1)}, f32[3,32,128]{2,1,0:T(8,128)S(1)}) custom-call(f32[264,128]{1,0:T(8,128)S(1)} %shard_map.46.refs_0_.refs_4_), custom_call_target="tpu_custom_call" | custom-call | flops 1 | bytes 1 | tf_op jit(solution)/shard_map/pallas_call | solution.py:289
  7.3 0.0 collective-permute-done.refs_0_.refs_5_
  7.3 3.4 %collective-permute-start.3 = (f32[264,128]{1,0:T(8,128)S(1)}, f32[264,128]{1,0:T(8,128)S(1)}, u32[]{:S(2)}, u32[]{:S(2)}) collective-permute-start(f32[264,128]{1,0:T(8,128)S(1)} %collective-permute-done.refs_0_.refs_5_), channel_id=1, source_target_pairs={{0,1},{1,0},{2,3},{3,2},{4,5},{5,4},{6,7},{7,6},{8,9},{9,8},{10,11... | collective-permute-start | bytes 405512 | tf_op jit(solution)/shard_map/ppermute | solution.py:26
  10.7 1.1 %collective-permute-start.6 = (f32[264,128]{1,0:T(8,128)S(1)}, f32[264,128]{1,0:T(8,128)S(1)}, u32[]{:S(2)}, u32[]{:S(2)}) collective-permute-start(f32[264,128]{1,0:T(8,128)S(1)} %collective-permute-done.refs_0_.refs_5_), channel_id=1, source_target_pairs={{1,2},{2,1},{3,0},{0,3},{5,6},{6,5},{7,4},{4,7},{9,10},{10,9},{11,... | collective-permute-start | bytes 405512 | tf_op jit(solution)/shard_map/ppermute | solution.py:26
  11.8 0.0 collective-permute-done.4.refs_1_
  11.8 0.5 %collective-permute-start.5 = (f32[256,128]{1,0:T(8,128)S(1)}, f32[256,128]{1,0:T(8,128)S(1)}, u32[]{:S(2)}, u32[]{:S(2)}) collective-permute-start(f32[256,128]{1,0:T(8,128)S(1)} %collective-permute-done.4.refs_1_), channel_id=1, source_target_pairs={{0,1},{1,0},{2,3},{3,2},{4,5},{5,4},{6,7},{7,6},{8,9},{9,8},{10,11... | collective-permute-start | bytes 393224 | tf_op jit(solution)/shard_map/ppermute | solution.py:26
  12.3 0.0 collective-permute-done.1.refs_1_.refs_6_
  12.3 0.2 collective-permute-start.8
  13.2 0.0 collective-permute-done.2.refs_2_.refs_7_
  13.2 0.8 %shard_map.48 = (bf16[576,32,128]{2,1,0:T(8,128)(2,1)S(1)}, bf16[576,16,128]{2,1,0:T(8,128)(2,1)S(1)}) custom-call(bf16[576,32,128]{2,1,0:T(8,128)(2,1)S(1)} %get-tuple-element.21.feature_in, bf16[576,16,128]{2,1,0:T(8,128)(2,1)S(1)} %get-tuple-element.22.moment_in, ...), custom_call_target="tpu_custom_call", output_to_operand_aliasing={{0}: (0, {}), {1}: (1, {})} | custom-call | flops 1 | bytes 1 | tf_op jit(solution)/shard_map/pallas_call | solution.py:307
  14.0 0.0 collective-permute-done.5.refs_2_
  14.0 0.0 collective-permute-done.3.refs_0_
  14.0 2.9 %collective-permute-done.6.refs_3_ = f32[264,128]{1,0:T(8,128)S(1)} collective-permute-done((f32[264,128]{1,0:T(8,128)S(1)}, f32[264,128]{1,0:T(8,128)S(1)}, u32[]{:S(2)}, u32[]{:S(2)}) %collective-permute-start.6) | collective-permute-done | bytes 135200 | tf_op jit(solution)/shard_map/ppermute | solution.py:26
  16.8 1.0 %shard_map.49 = (bf16[576,32,128]{2,1,0:T(8,128)(2,1)S(1)}, bf16[576,16,128]{2,1,0:T(8,128)(2,1)S(1)}, f32[128]{0:T(128)S(1)}, f32[128]{0:T(128)S(1)}) custom-call(bf16[576,32,128]{2,1,0:T(8,128)(2,1)S(1)} %get-tuple-element.25.feature_in, bf16[576,16,128]{2,1,0:T(8,128)(2,1)S(1)} %get-tuple-element.26.moment_in, ...), custom_call_target="tpu_custom_call", output_to_operand_aliasing={{0}: (0, {}), {1}: (1, {})} | custom-call | flops 1 | bytes 1 | tf_op jit(solution)/shard_map/pallas_call | solution.py:319
  17.8 0.1 collective-permute-start.7
  17.9 0.8 %collective-permute-done.8.refs_0_ = f32[256,128]{1,0:T(8,128)S(1)} collective-permute-done((f32[256,128]{1,0:T(8,128)S(1)}, f32[256,128]{1,0:T(8,128)S(1)}, u32[]{:S(2)}, u32[]{:S(2)}) %collective-permute-start.8) | collective-permute-done | bytes 131104 | tf_op jit(solution)/shard_map/ppermute | solution.py:26
  18.7 0.3 shard_map.50
  19.0 0.1 collective-permute-done.7
  19.0 1.3 %collective-permute-start.9 = (f32[128]{0:T(128)S(1)}, f32[128]{0:T(128)S(1)}, u32[]{:S(2)}, u32[]{:S(2)}) collective-permute-start(f32[128]{0:T(128)S(1)} %add_add_fusion.tie), channel_id=1, source_target_pairs={{0,8},{4,12},{8,0},{12,4},{16,24},{20,28},{24,16},{28,20},{1,9},{5... | collective-permute-start | bytes 1544 | tf_op jit(solution)/shard_map/ppermute | solution.py:30
  20.3 0.0 copy-done.1
  20.3 5.4 %shard_map.51.refs_0_ = f32[3,16,128]{2,1,0:T(8,128)S(1)} custom-call(s32[16,32]{1,0:T(8,128)S(1)} %bitcast.9, f32[128]{0:T(128)S(1)} %add_add_fusion.tie, s32[1,1]{1,0:T(1,128)S(6)} %copy.17.limit, bf16[576,32,128]{2,1,0:T(8,128)(2,1)S(1)} %get-tuple-element.32.feature, bf16[576,16,128]{2,1,0:T(8,128)(2,1)S(1)} %get-tuple-element.34.moment, ...), custom_call_target="tpu_custom_call" | custom-call | flops 83886080 | bytes 24576 | tf_op jit(solution)/shard_map/pallas_call | solution.py:349
  25.8 0.0 collective-permute-done.9
  25.8 1.4 %collective-permute-start.10 = (f32[128]{0:T(128)S(1)}, f32[128]{0:T(128)S(1)}, u32[]{:S(2)}, u32[]{:S(2)}) collective-permute-start(f32[128]{0:T(128)S(1)} %add.11.tie.some_mass), channel_id=1, source_target_pairs={{0,16},{4,20},{8,24},{12,28},{16,0},{20,4},{24,8},{28,12},{1,17},{... | collective-permute-start | bytes 1544 | tf_op jit(solution)/shard_map/ppermute | solution.py:30
  27.2 5.4 %shard_map.52.refs_1_ = f32[3,16,128]{2,1,0:T(8,128)S(1)} custom-call(s32[16,32]{1,0:T(8,128)S(1)} %bitcast.10, f32[128]{0:T(128)S(1)} %add.11.tie.some_mass, s32[1,1]{1,0:T(1,128)S(6)} %copy.17.limit, bf16[576,32,128]{2,1,0:T(8,128)(2,1)S(1)} %get-tuple-element.32.feature, bf16[576,16,128]{2,1,0:T(8,128)(2,1)S(1)} %get-tuple-element.34.moment, ...), custom_call_target="tpu_custom_call" | custom-call | flops 83886080 | bytes 24576 | tf_op jit(solution)/shard_map/pallas_call | solution.py:349
  32.6 0.0 collective-permute-done.10.more_mass
  32.6 0.8 %shard_map.53 = f32[3,32,128]{2,1,0:T(8,128)} custom-call(f32[128]{0:T(128)S(1)} %add.11.tie.some_mass, f32[128]{0:T(128)S(1)} %collective-permute-done.10.more_mass, s32[1,1]{1,0:T(1,128)S(6)} %copy.17.limit, f32[3,32,128]{2,1,0:T(8,128)S(1)} %get-tuple-element.23.centre, f32[3,16,128]{2,1,0:T(8,128)S(1)} %shard_map.51.refs_0_, ...), custom_call_target="tpu_custom_call" | custom-call | tf_op jit(solution)/shard_map/pallas_call | solution.py:377
  (4 shorter events, 0.0 us)
Async XLA Ops:
  0.0 0.7 %copy-start = (s32[1,1,64]{2,1,0:T(1,128)S(1)}, s32[1,1,64]{2,1,0:T(1,128)}, u32[]{:S(2)}) copy-start(s32[1,1,64]{2,1,0:T(1,128)} %param.7) | copy-start | bytes 772
  1.8 5.5 %collective-permute-start = (f32[264,128]{1,0:T(8,128)S(1)}, f32[264,128]{1,0:T(8,128)S(1)}, u32[]{:S(2)}, u32[]{:S(2)}) collective-permute-start(f32[264,128]{1,0:T(8,128)S(1)} %shard_map.46.refs_0_.refs_4_), channel_id=1, source_target_pairs={{0,4},{4,0},{8,12},{12,8},{16,20},{20,16},{24,28},{28,24},{1,5},{5... | collective-permute-start | bytes 405512 | tf_op jit(solution)/shard_map/ppermute | solution.py:26
  1.9 10.4 %collective-permute-start.1 = (f32[264,128]{1,0:T(8,128)S(1)}, f32[264,128]{1,0:T(8,128)S(1)}, u32[]{:S(2)}, u32[]{:S(2)}) collective-permute-start(f32[264,128]{1,0:T(8,128)S(1)} %shard_map.46.refs_0_.refs_4_), channel_id=1, source_target_pairs={{0,1},{1,0},{2,3},{3,2},{4,5},{5,4},{6,7},{7,6},{8,9},{9,8},{10,11... | collective-permute-start | bytes 405512 | tf_op jit(solution)/shard_map/ppermute | solution.py:26
  2.6 9.2 %collective-permute-start.4 = (f32[256,128]{1,0:T(8,128)}, f32[256,128]{1,0:T(8,128)S(1)}, u32[]{:S(2)}, u32[]{:S(2)}) collective-permute-start(f32[256,128]{1,0:T(8,128)} %bitcast.blocks), channel_id=1, source_target_pairs={{4,8},{8,4},{12,16},{16,12},{20,24},{24,20},{28,0},{0,28},{5,9},{9... | collective-permute-start | bytes 393224 | tf_op jit(solution)/shard_map/ppermute | solution.py:26
  5.3 7.9 %collective-permute-start.2 = (f32[264,128]{1,0:T(8,128)S(1)}, f32[264,128]{1,0:T(8,128)S(1)}, u32[]{:S(2)}, u32[]{:S(2)}) collective-permute-start(f32[264,128]{1,0:T(8,128)S(1)} %shard_map.46.refs_0_.refs_4_), channel_id=1, source_target_pairs={{1,2},{2,1},{3,0},{0,3},{5,6},{6,5},{7,4},{4,7},{9,10},{10,9},{11,... | collective-permute-start | bytes 405512 | tf_op jit(solution)/shard_map/ppermute | solution.py:26
  7.3 6.7 %collective-permute-start.3 = (f32[264,128]{1,0:T(8,128)S(1)}, f32[264,128]{1,0:T(8,128)S(1)}, u32[]{:S(2)}, u32[]{:S(2)}) collective-permute-start(f32[264,128]{1,0:T(8,128)S(1)} %collective-permute-done.refs_0_.refs_5_), channel_id=1, source_target_pairs={{0,1},{1,0},{2,3},{3,2},{4,5},{5,4},{6,7},{7,6},{8,9},{9,8},{10,11... | collective-permute-start | bytes 405512 | tf_op jit(solution)/shard_map/ppermute | solution.py:26
  10.7 6.1 %collective-permute-start.6 = (f32[264,128]{1,0:T(8,128)S(1)}, f32[264,128]{1,0:T(8,128)S(1)}, u32[]{:S(2)}, u32[]{:S(2)}) collective-permute-start(f32[264,128]{1,0:T(8,128)S(1)} %collective-permute-done.refs_0_.refs_5_), channel_id=1, source_target_pairs={{1,2},{2,1},{3,0},{0,3},{5,6},{6,5},{7,4},{4,7},{9,10},{10,9},{11,... | collective-permute-start | bytes 405512 | tf_op jit(solution)/shard_map/ppermute | solution.py:26
  11.8 2.1 %collective-permute-start.5 = (f32[256,128]{1,0:T(8,128)S(1)}, f32[256,128]{1,0:T(8,128)S(1)}, u32[]{:S(2)}, u32[]{:S(2)}) collective-permute-start(f32[256,128]{1,0:T(8,128)S(1)} %collective-permute-done.4.refs_1_), channel_id=1, source_target_pairs={{0,1},{1,0},{2,3},{3,2},{4,5},{5,4},{6,7},{7,6},{8,9},{9,8},{10,11... | collective-permute-start | bytes 393224 | tf_op jit(solution)/shard_map/ppermute | solution.py:26
  12.3 6.4 %collective-permute-start.8 = (f32[256,128]{1,0:T(8,128)S(1)}, f32[256,128]{1,0:T(8,128)S(1)}, u32[]{:S(2)}, u32[]{:S(2)}) collective-permute-start(f32[256,128]{1,0:T(8,128)S(1)} %collective-permute-done.4.refs_1_), channel_id=1, source_target_pairs={{1,2},{2,1},{3,0},{0,3},{5,6},{6,5},{7,4},{4,7},{9,10},{10,9},{11,... | collective-permute-start | bytes 393224 | tf_op jit(solution)/shard_map/ppermute | solution.py:26
  17.8 1.2 %collective-permute-start.7 = (f32[128]{0:T(128)S(1)}, f32[128]{0:T(128)S(1)}, u32[]{:S(2)}, u32[]{:S(2)}) collective-permute-start(f32[128]{0:T(128)S(1)} %get-tuple-element.29), channel_id=1, source_target_pairs={{0,1},{1,0},{2,3},{3,2},{4,5},{5,4},{6,7},{7,6},{8,9},{9,8},{10,11... | collective-permute-start | bytes 1544 | tf_op jit(solution)/shard_map/ppermute | solution.py:30
  18.7 1.6 %copy-start.1 = (s32[1,1,32,16]{2,3,1,0:T(8,128)S(1)}, s32[1,1,32,16]{2,3,1,0:T(8,128)}, u32[]{:S(2)}) copy-start(s32[1,1,32,16]{2,3,1,0:T(8,128)} %param.6) | copy-start | bytes 6148
  19.0 6.7 %collective-permute-start.9 = (f32[128]{0:T(128)S(1)}, f32[128]{0:T(128)S(1)}, u32[]{:S(2)}, u32[]{:S(2)}) collective-permute-start(f32[128]{0:T(128)S(1)} %add_add_fusion.tie), channel_id=1, source_target_pairs={{0,8},{4,12},{8,0},{12,4},{16,24},{20,28},{24,16},{28,20},{1,9},{5... | collective-permute-start | bytes 1544 | tf_op jit(solution)/shard_map/ppermute | solution.py:30
  25.8 6.8 %collective-permute-start.10 = (f32[128]{0:T(128)S(1)}, f32[128]{0:T(128)S(1)}, u32[]{:S(2)}, u32[]{:S(2)}) collective-permute-start(f32[128]{0:T(128)S(1)} %add.11.tie.some_mass), channel_id=1, source_target_pairs={{0,16},{4,20},{8,24},{12,28},{16,0},{20,4},{24,8},{28,12},{1,17},{... | collective-permute-start | bytes 1544 | tf_op jit(solution)/shard_map/ppermute | solution.py:30
